TPU v7x, 256 devices: a whole 4x4x8 slice. The times are simulated.
256 devices in a mesh: dp: 64 (over x, z, y_hi), seq: 4 (over y_lo, core).
Axes of the slice: x: 4, y: 4 (y_hi: 2, y_lo: 2; y = y_hi * 2 + y_lo), z: 8, core: 2. Of those that a mesh axis runs over, the one named last changes fastest.
Arguments:
- layer_input: bfloat16 [64, 512, 5120], P('dp', 'seq'), may hold values from -16 to 16
- query_states: bfloat16 [64, 512, 2560], P('dp', 'seq'), may hold values from -7 to 7
- key_states: bfloat16 [64, 512, 512], P('dp', 'seq'), may hold values from -7 to 7
- value_states: bfloat16 [64, 512, 512], P('dp', 'seq'), may hold values from -6 to 6
- output_grads: bfloat16 [64, 512, 2560], P('dp', 'seq'), may hold values from -24 to 24
- doc_lengths: int32 [64, 6], P('dp'), may hold values from 1 to 256, 512 in all within a row
Outputs:
- query_grads: bfloat16 [64, 512, 2560], P('dp', 'seq')
- key_weight_grads: float32 [5120, 512], P('dp', 'seq')
- value_weight_grads: float32 [5120, 512], P('dp', 'seq')
Inputs may be any that keep to these rules, and one draw needn't show every extreme that they name: `doc_lengths`: each row holds the lengths of the 6 documents of one sequence in order; they sum to 512 and the longest has exactly 256 tokens.
All inputs are finite; a program needn't handle non-finite values.
Results may differ from a plain program's by a relative error of at most 0.018.
Values may be sent and summed in bfloat16 or wider, within the bound.
A program may use at most 128 MiB of HBM per device.

v0:
```python
from functools import reduce

import jax
import jax.numpy as jnp
from jax import lax
from jax.sharding import PartitionSpec as P

HD = 128
KVH = 4
GROUP = 5


NEG_FILL = -1e30


def document_ids(length_row, count):
    doc_ends = jnp.cumsum(length_row)
    positions = jnp.arange(count, dtype=jnp.int32)
    return jnp.sum((positions[:, None] >= doc_ends[None, :]).astype(jnp.int32), axis=1)


def attend_back(query_blocks, grad_blocks, key_heads, value_heads, doc_rows, doc_keys, offset):
    query_rows, groups, group_heads, head_width = query_blocks.shape
    key_rows = key_heads.shape[0]
    score_scale = head_width ** (-0.5)
    row_block = min(512, query_rows)
    key_grads = jnp.zeros((key_rows, groups, head_width), jnp.float32)
    value_grads = jnp.zeros((key_rows, groups, head_width), jnp.float32)
    row_places = offset + jnp.arange(row_block, dtype=jnp.int32)
    last_row = offset + row_block - 1
    key_limit = last_row + 1
    key_spans = list(range(0, key_limit, key_limit))
    tile_flags = []
    for key_first in key_spans:
        tile_flags.append(True)
    score_tiles = []
    for key_first, tile_flag in zip(key_spans, tile_flags):

        def scored(key_first=key_first):
            raw_scores = (
                jnp.einsum(
                    "qghd,kgd->ghqk", query_blocks, key_heads, preferred_element_type=jnp.float32
                )
                * score_scale
            )
            key_places = key_first + jnp.arange(key_limit, dtype=jnp.int32)
            allowed = (doc_rows[:, None] == doc_keys[None, :]) & (
                key_places[None, :] <= row_places[:, None]
            )
            return jnp.where(allowed, raw_scores, NEG_FILL)

        score_tiles.append(scored())
    row_max = reduce(jnp.maximum, [jnp.max(tile_scores, axis=-1) for tile_scores in score_tiles])
    shifted = [jnp.exp(tile_scores - row_max[..., None]) for tile_scores in score_tiles]
    row_sum = reduce(jnp.add, [jnp.sum(shifted_tile, axis=-1) for shifted_tile in shifted])
    prob_tiles = [shifted_tile / row_sum[..., None] for shifted_tile in shifted]
    dprob_tiles = []
    for key_first, tile_flag in zip(key_spans, tile_flags):

        def projected(key_first=key_first):
            return jnp.einsum(
                "qghd,kgd->ghqk", grad_blocks, value_heads, preferred_element_type=jnp.float32
            )

        dprob_tiles.append(projected())
    row_delta = reduce(
        jnp.add,
        [
            jnp.sum(prob_tile * dprob_tile, axis=-1)
            for prob_tile, dprob_tile in zip(prob_tiles, dprob_tiles)
        ],
    )
    query_total = jnp.zeros((row_block, groups, group_heads, head_width), jnp.float32)
    for key_first, tile_flag, prob_tile, dprob_tile in zip(
        key_spans, tile_flags, prob_tiles, dprob_tiles
    ):
        dscores = (prob_tile * (dprob_tile - row_delta[..., None]) * score_scale).astype(
            jnp.bfloat16
        )
        prob_bf = prob_tile.astype(jnp.bfloat16)
        key_tile = key_heads

        def query_term(dscores=dscores, key_tile=key_tile):
            return jnp.einsum(
                "ghqk,kgd->qghd", dscores, key_tile, preferred_element_type=jnp.float32
            )

        def key_term(dscores=dscores):
            return jnp.einsum(
                "ghqk,qghd->kgd", dscores, query_blocks, preferred_element_type=jnp.float32
            )

        def value_term(prob_bf=prob_bf):
            return jnp.einsum(
                "ghqk,qghd->kgd", prob_bf, grad_blocks, preferred_element_type=jnp.float32
            )

        query_total = query_term()
        key_grads = key_grads.at[key_first : key_first + key_limit].add(key_term())
        value_grads = value_grads.at[key_first : key_first + key_limit].add(value_term())
    query_parts = query_total.astype(jnp.bfloat16)
    return (query_parts, key_grads, value_grads)


def token_weights(rows_input, key_tokens, value_tokens):
    token_count, model_width = rows_input.shape
    head_count = key_tokens.shape[1] // HD
    paired = jnp.stack(
        (
            key_tokens.reshape(token_count, head_count, HD),
            value_tokens.reshape(token_count, head_count, HD),
        ),
        axis=2,
    )
    paired = paired.reshape(token_count, head_count * 2 * HD)
    row_share = lax.psum_scatter(
        lax.dot_general(
            rows_input, paired, (((0,), (0,)), ((), ())), preferred_element_type=jnp.float32
        ),
        "dp",
        scatter_dimension=0,
        tiled=True,
    )
    head_share = lax.psum_scatter(
        row_share.astype(jnp.bfloat16), "seq", scatter_dimension=1, tiled=True
    ).astype(jnp.float32)
    owned_rows = head_share.shape[0]
    local_heads = head_share.shape[1] // (2 * HD)
    head_share = head_share.reshape(owned_rows, local_heads, 2, HD) / lax.axis_size("dp")
    return (
        head_share[:, :, 0, :].reshape(owned_rows, local_heads * HD),
        head_share[:, :, 1, :].reshape(owned_rows, local_heads * HD),
    )


def per_device(layer_input, query_states, key_states, value_states, output_grads, doc_lengths):
    token_count = layer_input.shape[1]
    query_width = query_states.shape[2]
    kv_width = key_states.shape[2]
    seq_count = lax.axis_size("seq")
    seq_length = token_count * seq_count
    rows_input = layer_input[0]
    doc_full = document_ids(doc_lengths[0], seq_length)
    heads_here = KVH // seq_count
    query_split = query_states[0].reshape(token_count, seq_count, heads_here, GROUP * HD)
    key_split = key_states[0].reshape(token_count, seq_count, heads_here, HD)
    value_split = value_states[0].reshape(token_count, seq_count, heads_here, HD)
    grad_split = output_grads[0].reshape(token_count, seq_count, heads_here, GROUP * HD)
    query_heads = lax.all_to_all(query_split, "seq", split_axis=1, concat_axis=0, tiled=True)
    key_heads = lax.all_to_all(key_split, "seq", split_axis=1, concat_axis=0, tiled=True)
    value_heads = lax.all_to_all(value_split, "seq", split_axis=1, concat_axis=0, tiled=True)
    grad_heads = lax.all_to_all(grad_split, "seq", split_axis=1, concat_axis=0, tiled=True)
    item_count = query_heads.shape[2]
    query_grad, key_grad, value_grad = attend_back(
        query_heads.reshape(seq_length, item_count, GROUP, HD),
        grad_heads.reshape(seq_length, item_count, GROUP, HD),
        key_heads.reshape(seq_length, item_count, HD),
        value_heads.reshape(seq_length, item_count, HD),
        doc_full,
        doc_full,
        0,
    )
    query_heads = query_grad.reshape(seq_length, 1, item_count, GROUP * HD)
    key_heads = key_grad.astype(jnp.bfloat16).reshape(seq_length, 1, item_count, HD)
    value_heads = value_grad.astype(jnp.bfloat16).reshape(seq_length, 1, item_count, HD)
    query_back, key_back, value_back = (
        lax.all_to_all(query_heads, "seq", split_axis=0, concat_axis=1, tiled=True),
        lax.all_to_all(key_heads, "seq", split_axis=0, concat_axis=1, tiled=True),
        lax.all_to_all(value_heads, "seq", split_axis=0, concat_axis=1, tiled=True),
    )
    query_tokens = query_back.reshape(token_count, query_width)
    key_weight_grads, value_weight_grads = token_weights(
        rows_input,
        key_back.reshape(token_count, kv_width),
        value_back.reshape(token_count, kv_width),
    )
    return (query_tokens.reshape(1, token_count, query_width), key_weight_grads, value_weight_grads)


def solution(mesh):
    return jax.shard_map(
        per_device,
        mesh=mesh,
        in_specs=(
            P("dp", "seq", None),
            P("dp", "seq", None),
            P("dp", "seq", None),
            P("dp", "seq", None),
            P("dp", "seq", None),
            P("dp", None),
        ),
        out_specs=(P("dp", "seq", None), P("dp", "seq"), P("dp", "seq")),
        check_vma=False,
    )
```

profile of v0, /device:TPU:9, one launch (start us, length us, event | category | flops | bytes accessed | tf_op | source)
XLA Modules:
  0.0 608.2 jit_solution(12547611537715539850)
XLA Ops:
  7.2 2.3 copy.91
  9.5 6.0 all-to-all-start.1
  15.4 2.2 copy.96
  17.6 6.2 %all-to-all-done.1 = bf16[128,4,1,640]{0,3,2,1:T(8,128)(2,1)S(1)} async-done(((bf16[128,4,1,640]{0,3,2,1:T(8,128)(2,1)}), bf16[128,4,1,640]{0,3,2,1:T(8,128)(2,1)S(1)}, u32[]{:S(2)}, u32[]{:S(2)}) %all-to-all-start.1) | async-done | bytes 655392 | tf_op jit(solution)/shard_map/all_to_all | solution.py:149
  23.8 6.0 all-to-all-start.3
  31.0 7.3 %all-to-all-done.3 = bf16[128,4,1,640]{0,3,2,1:T(8,128)(2,1)} async-done(((bf16[128,4,1,640]{0,3,2,1:T(8,128)(2,1)}), bf16[128,4,1,640]{0,3,2,1:T(8,128)(2,1)}, u32[]{:S(2)}, u32[]{:S(2)}) %all-to-all-start.3) | async-done | bytes 655392 | tf_op jit(solution)/shard_map/all_to_all | solution.py:152
  38.3 5.2 all-to-all-start
  45.9 1.6 reshape.193
  47.5 1.6 copy.97
  50.2 3.9 all-to-all-start.2
  57.5 1.5 fusion.21
  60.9 3.3 all-to-all-start.6
  64.2 4.8 fusion
  69.0 1.8 fusion.7
  70.9 1.5 copy-done.3
  74.6 3.3 all-to-all-start.5
  78.3 2.4 all-to-all-done.5
  81.1 8.5 %convolution_bitcast_fusion = f32[5120,1024]{0,1:T(8,128)} fusion(bf16[128,1024]{0,1:T(8,128)(2,1)S(1)} %bitcast.155, bf16[1,128,5120]{2,1,0:T(8,128)(2,1)S(1)} %copy-done), kind=kOutput, calls=%fused_computation | convolution fusion | flops 1342177280 | bytes 22544384 | tf_op jit(solution)/shard_map/dot_general | solution.py:117
  89.6 21.3 %copy.118 = f32[5120,1024]{1,0:T(8,128)} copy(f32[5120,1024]{0,1:T(8,128)} %convolution_bitcast_fusion) | data formatting | bytes 41943040
  111.0 2.3 convolution_convert_fusion
  115.7 5.4 all-to-all-start.4
  121.1 456.6 %reduce-scatter.7.cloned.1.call-done = f32[80,1024]{1,0:T(8,128)} async-done(((f32[5120,1024]{1,0:T(8,128)}), f32[80,1024]{1,0:T(8,128)}) %reduce-scatter.7.cloned.1.call-update) | async-done | bytes 327696
  577.7 1.8 copy.119
  581.8 17.3 %reduce-scatter.5.cloned.1.call-done = bf16[80,256]{0,1:T(8,128)(2,1)} async-done(((bf16[80,1024]{0,1:T(8,128)(2,1)}), bf16[80,256]{0,1:T(8,128)(2,1)}) %reduce-scatter.5.cloned.1.call-update) | async-done | bytes 40976 | tf_op jit(solution)/shard_map/reduce_scatter | solution.py:124
  (66 shorter events, 19.7 us)
Async XLA Ops:
  7.2 73.9 %copy-start = (bf16[1,128,5120]{2,1,0:T(8,128)(2,1)S(1)}, bf16[1,128,5120]{2,1,0:T(8,128)(2,1)}, u32[]{:S(2)}) copy-start(bf16[1,128,5120]{2,1,0:T(8,128)(2,1)} %param.14) | copy-start | bytes 3932164
  7.2 22.6 %copy-start.5 = (bf16[1,128,512]{2,1,0:T(8,128)(2,1)S(1)}, bf16[1,128,512]{2,1,0:T(8,128)(2,1)}, u32[]{:S(2)}) copy-start(bf16[1,128,512]{2,1,0:T(8,128)(2,1)} %param.16) | copy-start | bytes 393220
  7.2 23.5 %copy-start.9 = (s32[1,6]{1,0:T(1,128)S(1)}, s32[1,6]{1,0:T(1,128)}, u32[]{:S(2)}) copy-start(s32[1,6]{1,0:T(1,128)} %param.19) | copy-start | bytes 76
  7.2 36.5 %copy-start.6 = (bf16[1,128,512]{2,1,0:T(8,128)(2,1)S(1)}, bf16[1,128,512]{2,1,0:T(8,128)(2,1)}, u32[]{:S(2)}) copy-start(bf16[1,128,512]{2,1,0:T(8,128)(2,1)} %param.17) | copy-start | bytes 393220
  9.5 14.3 %all-to-all-start.1 = ((bf16[128,4,1,640]{0,3,2,1:T(8,128)(2,1)}), bf16[128,4,1,640]{0,3,2,1:T(8,128)(2,1)S(1)}, u32[]{:S(2)}, u32[]{:S(2)}) async-start(bf16[128,4,1,640]{0,3,2,1:T(8,128)(2,1)} %bitcast.7), calls=%async_computation.1 | async-start | bytes 1310720 | tf_op jit(solution)/shard_map/all_to_all | solution.py:149
  23.8 14.5 %all-to-all-start.3 = ((bf16[128,4,1,640]{0,3,2,1:T(8,128)(2,1)}), bf16[128,4,1,640]{0,3,2,1:T(8,128)(2,1)}, u32[]{:S(2)}, u32[]{:S(2)}) async-start(bf16[128,4,1,640]{0,3,2,1:T(8,128)(2,1)} %bitcast.17), calls=%async_computation.3 | async-start | bytes 1310720 | tf_op jit(solution)/shard_map/all_to_all | solution.py:152
  38.3 11.9 %all-to-all-start = ((bf16[128,4,1,128]{3,0,2,1:T(8,128)(2,1)}), bf16[128,4,1,128]{3,0,2,1:T(8,128)(2,1)S(1)}, u32[]{:S(2)}, u32[]{:S(2)}) async-start(bf16[128,4,1,128]{3,0,2,1:T(8,128)(2,1)} %copy.90), calls=%async_computation | async-start | bytes 262144 | tf_op jit(solution)/shard_map/all_to_all | solution.py:150
  50.2 10.7 %all-to-all-start.2 = ((bf16[128,4,1,128]{3,0,2,1:T(8,128)(2,1)}), bf16[128,4,1,128]{3,0,2,1:T(8,128)(2,1)}, u32[]{:S(2)}, u32[]{:S(2)}) async-start(bf16[128,4,1,128]{3,0,2,1:T(8,128)(2,1)} %copy.95), calls=%async_computation.2 | async-start | bytes 262144 | tf_op jit(solution)/shard_map/all_to_all | solution.py:151
  54.1 3.3 copy-start.4
  55.2 2.3 copy-start.2
  57.5 1.5 copy-start.7
  60.2 8.8 %slice-start = ((s8[5242880]{0:T(1024)(128)(4,1)}), s8[1048576]{0:T(1024)(128)(4,1)S(1)}, s32[]{:S(2)}) async-start(s8[5242880]{0:T(1024)(128)(4,1)} %bitcast.149), calls=%async_computation.11 | async-start | bytes 2097152
  60.9 13.7 %all-to-all-start.6 = ((bf16[4,2,8192]{2,1,0:T(2,128)(2,1)}), bf16[4,2,8192]{2,1,0:T(2,128)(2,1)S(1)}, u32[]{:S(2)}, u32[]{:S(2)}) async-start(bf16[4,2,8192]{2,1,0:T(2,128)(2,1)} %reshape.211), calls=%async_computation.6 | async-start | bytes 262144 | tf_op jit(solution)/shard_map/all_to_all | solution.py:169
  64.2 4.8 slice-start.1
  64.2 4.8 copy-start.8
  70.9 1.5 copy-start.3
  74.6 6.1 all-to-all-start.5
  78.0 499.8 %reduce-scatter.7.cloned.1.call-start = ((), (), s32[]{:S(2)}) async-start(), calls=%async_computation.10 | async-start | bytes 21299200
  114.4 486.9 %copy-start.1 = (bf16[1,128,5120]{2,1,0:T(8,128)(2,1)S(1)}, bf16[1,128,5120]{2,1,0:T(8,128)(2,1)}, u32[]{:S(2)}) copy-start(bf16[1,128,5120]{2,1,0:T(8,128)(2,1)} %param.14) | copy-start | bytes 3932164
  115.7 463.8 %all-to-all-start.4 = ((bf16[4,2,40960]{2,1,0:T(2,128)(2,1)}), bf16[4,2,40960]{2,1,0:T(2,128)(2,1)S(1)}, u32[]{:S(2)}, u32[]{:S(2)}) async-start(bf16[4,2,40960]{2,1,0:T(2,128)(2,1)} %reshape.209), calls=%async_computation.4 | async-start | bytes 1310720 | tf_op jit(solution)/shard_map/all_to_all | solution.py:167
  121.1 478.0 %reduce-scatter.5.cloned.1.call-start = ((), (), s32[]{:S(2)}) async-start(), calls=%async_computation.9 | async-start | bytes 327680 | tf_op jit(solution)/shard_map/reduce_scatter | solution.py:124
Sparse Core Ops, SparseCore 0:
  111.1 466.6 reduce-scatter.6
  580.2 18.7 reduce-scatter.4
where the time goes:
time: 611 us; the launch traced here: 608 us
  waiting for transfers between devices  490 us (80%)
  local copies, waits for them, and re-layouts  44.9 us (7%)
  starting transfers between devices  33.4 us (5%)
  matrix products  19 us (3%)
  between operations  14.4 us (2%)
  other arithmetic  6.75 us (1%)
    unnamed x3, waiting for transfers between devices  457 us
    unnamed x43, local copies, waits for them, and re-layouts  36.8 us
    reduce_scatter x1, waiting for transfers between devices, token_weights(): lax.psum_scatter(row_share.astype(jnp.bfloat16), 'seq', scatter_dimension...  17.3 us
  transfers between devices with their start and end apart: 9, of which 5 were waited for; matrix products, arithmetic and copies ran while one was open for 5% of the time, Pallas kernels for 0%

commit v1 on v0

v1 whole, which is shorter than its diff:
```python
import jax
import jax.numpy as jnp
from jax import lax
from jax.experimental import pallas as pl
from jax.experimental.pallas import tpu as pltpu
from jax.sharding import PartitionSpec as P

HD = 128
KVH = 4
GROUP = 5
TOK = 128
D = 5120
XW = D // 4
NX, NY, NZ = 4, 4, 8
ROWS = 80
LOG2E = 1.4426950408889634
SCALE = HD ** (-0.5)
MESH = pl.DeviceIdType.MESH
F32 = jnp.float32
BF16 = jnp.bfloat16


def kernel(
    doc_ref, x_hbm, q_hbm, k_hbm, v_hbm, do_hbm,
    dq_hbm, wk_ref, wv_ref,
    xin, qin, doin, kv, bias, ds_s, pb_s, dq_s, xt_send, xt_all,
    part_own, part_send, part_recv, kvout, kv_all, dw, zsend, zrecv, ysend, yrecv,
    ld_sem, kv_ss, kv_rs, x_ss, x_rs, xf_ss, xf_rs, p_ss, p_rs,
    ag_ss, ag_rs, rl_ss, rl_rs, z_ss, z_rs, y_ss, y_rs, out_sem,
):
    dp = lax.axis_index("dp")
    sq = lax.axis_index("seq")
    x = dp // 16
    z = (dp // 2) % 8
    yh = dp % 2
    yl = sq // 2
    c = sq % 2
    y = yh * 2 + yl

    def dev(xx, yy, zz, cc):
        return ((xx * 8 + zz) * 2 + yy // 2, (yy % 2) * 2 + cc)

    def seq_dev(delta):
        return (dp, (sq + delta) % 4)

    def rcopy(src, dst, ss, rs, device):
        return pltpu.make_async_remote_copy(
            src_ref=src, dst_ref=dst, send_sem=ss, recv_sem=rs,
            device_id=device, device_id_type=MESH,
        )

    loads = []
    for h in range(KVH):
        for i, ref in enumerate((k_hbm, v_hbm)):
            loads.append(pltpu.make_async_copy(
                ref.at[:, h * HD:(h + 1) * HD], kv.at[h, i, 256:384], ld_sem.at[h * 2 + i]))
    load_x = pltpu.make_async_copy(x_hbm, xin, ld_sem.at[8])
    load_q = pltpu.make_async_copy(q_hbm, qin, ld_sem.at[9])
    load_do = pltpu.make_async_copy(do_hbm, doin, ld_sem.at[10])
    for cp in loads:
        cp.start()
    load_x.start()
    load_q.start()
    load_do.start()

    barrier = pltpu.get_barrier_semaphore()
    xp, xm = (x + 1) % NX, (x + 3) % NX
    zp, zm = (z + 1) % NZ, (z + 7) % NZ
    out_y = (y + 3 + 2 * yl) % NY
    peers = [
        seq_dev(1), seq_dev(2), seq_dev(3),
        dev(xp, y, z, c), dev(xp, y, z, 1 - c), dev(xm, y, z, c), dev(xm, y, z, 1 - c),
        dev((x + 2) % NX, y, z, c),
        dev(x, y, zp, c), dev(x, y, zm, c),
        dev(x, out_y, z, c), dev(x, (y + 2) % NY, z, c),
    ]
    for peer in peers:
        pl.semaphore_signal(barrier, inc=1, device_id=peer, device_id_type=MESH)

    rows = lax.broadcasted_iota(jnp.int32, (TOK, 1), 0) + sq * TOK
    start = jnp.zeros((TOK, 1), jnp.int32)
    end = jnp.int32(0)
    for n in range(6):
        end = end + doc_ref[0, n]
        start = jnp.where(rows >= end, end, start)
    cols = lax.broadcasted_iota(jnp.int32, (TOK, 384), 1) + (sq - 2) * TOK
    bias[...] = jnp.where((cols >= start) & (cols <= rows), 0.0, -1e30).astype(F32)

    for cp in loads:
        cp.wait()
    pl.semaphore_wait(barrier, len(peers))

    sends = []
    for h in range(KVH):
        for delta in (1, 2):
            cp = rcopy(kv.at[h, :, 256:384], kv.at[h, :, (2 - delta) * TOK:(3 - delta) * TOK],
                       kv_ss.at[h, delta - 1], kv_rs.at[h, delta - 1], seq_dev(delta))
            cp.start()
            sends.append(cp)

    load_x.wait()

    def xt_slot(ref, d, rel):
        return ref.at[:, (d * 2 + rel) * TOK:(d * 2 + rel + 1) * TOK]

    for d in (1, 3, 2, 0):
        target = (x + d) % NX

        def turn(i, _, d=d, target=target):
            col = pl.multiple_of(target * XW + i * 128, 128)
            row = pl.multiple_of(i * 128, 128)
            tile = xin[:, pl.ds(col, 128)].T
            if d == 0:
                xt_all[pl.ds(row, 128), 0:128] = tile
            else:
                xt_send[d - 1, pl.ds(row, 128), :] = tile
            return 0

        lax.fori_loop(0, XW // 128, turn, 0)
        if d > 0:
            cp = rcopy(xt_send.at[d - 1], xt_slot(xt_all, d, 0), x_ss.at[d - 1], x_rs.at[d - 1],
                       dev(target, y, z, c))
            cp.start()
            sends.append(cp)

    def x_forward(d):
        cp = rcopy(xt_slot(xt_all, d, 0), xt_slot(xt_all, d, 1), xf_ss.at[d], xf_rs.at[d],
                   dev(x, y, z, 1 - c))
        cp.start()
        sends.append(cp)

    x_forward(0)
    load_q.wait()
    load_do.wait()

    out_copies = []

    def attention(h):
        for delta in (1, 2):
            rcopy(kv.at[h, :, 256:384], kv.at[h, :, (2 - delta) * TOK:(3 - delta) * TOK],
                  kv_ss.at[h, delta - 1], kv_rs.at[h, delta - 1], seq_dev(delta)).wait_recv()

        def head(g, _):
            col = pl.multiple_of((h * GROUP + g) * HD, HD)
            row = pl.multiple_of(g * TOK, TOK)
            kk = kv[h, 0]
            vv = kv[h, 1]
            s = lax.dot_general(qin[:, pl.ds(col, HD)], kk, (((1,), (1,)), ((), ())),
                                preferred_element_type=F32)
            s = s * (SCALE * LOG2E) + bias[...]
            m = jnp.max(s, axis=1, keepdims=True)
            e = jnp.exp2(s - m)
            p = e * (1.0 / jnp.sum(e, axis=1, keepdims=True))
            dpr = lax.dot_general(doin[:, pl.ds(col, HD)], vv, (((1,), (1,)), ((), ())),
                                  preferred_element_type=F32)
            delta_r = jnp.sum(p * dpr, axis=1, keepdims=True)
            ds = (p * (dpr - delta_r) * SCALE).astype(BF16)
            ds_s[pl.ds(row, TOK), :] = ds
            pb_s[pl.ds(row, TOK), :] = p.astype(BF16)
            dq = jnp.dot(ds, kk, preferred_element_type=F32)
            dq_s[:, pl.ds(col, HD)] = dq.astype(BF16)
            return 0

        lax.fori_loop(0, GROUP, head, 0)
        width = GROUP * HD
        cp = pltpu.make_async_copy(dq_s.at[:, h * width:(h + 1) * width],
                                   dq_hbm.at[:, h * width:(h + 1) * width], out_sem.at[h])
        cp.start()
        out_copies.append(cp)
        for i, (src, grads) in enumerate(((qin, ds_s), (doin, pb_s))):
            stacked = jnp.concatenate(
                [src[:, (h * GROUP + g) * HD:(h * GROUP + g + 1) * HD] for g in range(GROUP)],
                axis=0)
            t = lax.dot_general(stacked, grads[...], (((0,), (0,)), ((), ())),
                                preferred_element_type=F32)
            part_own[h, i] = t[:, 256:384]
            part_send[h, 0, i] = t[:, 128:256].astype(BF16)
            part_send[h, 1, i] = t[:, 0:128].astype(BF16)
        for delta in (1, 2):
            cp = part_copy(h, delta)
            cp.start()
            sends.append(cp)

    def part_copy(h, delta):
        return rcopy(part_send.at[h, delta - 1], part_recv.at[h, delta - 1],
                     p_ss.at[h, delta - 1], p_rs.at[h, delta - 1], seq_dev(4 - delta))

    def ag_rows(slot):
        return pl.ds(pl.multiple_of(slot * TOK, TOK), TOK)

    def finalize(h):
        j, core = h // 2, h % 2
        rel = (c + h) % 2
        for delta in (1, 2):
            part_copy(h, delta).wait_recv()
        for i in range(2):
            total = (part_own[h, i] + part_recv[h, 0, i].astype(F32)
                     + part_recv[h, 1, i].astype(F32))
            kvout[h, :, i * HD:(i + 1) * HD] = total.T.astype(BF16)

        for n, (d, xx) in enumerate(((1, xp), (3, xm))):
            cp = rcopy(kvout.at[h], kv_all.at[j, ag_rows(d * 2 + rel)],
                       ag_ss.at[h, n], ag_rs.at[j, n, rel], dev(xx, y, z, core))
            cp.start()
            sends.append(cp)

        @pl.when(rel == 1)
        def _():
            rcopy(kvout.at[h], kv_all.at[j, TOK:2 * TOK],
                  ag_ss.at[h, 2], ag_rs.at[j, 2, 1], dev(x, y, z, 1 - c)).start()

        @pl.when(rel == 0)
        def _():
            kv_all[j, 0:TOK] = kvout[h]

    def relay_copy(j, rel, n):
        half = slice(0, HD) if n == 0 else slice(HD, 2 * HD)
        d, xx = ((1, xp), (3, xm))[n]
        return rcopy(kv_all.at[j, (d * 2 + rel) * TOK:(d * 2 + rel + 1) * TOK, half],
                     kv_all.at[j, (4 + rel) * TOK:(5 + rel) * TOK, half],
                     rl_ss.at[j, rel, n], rl_rs.at[j, rel, n], dev(xx, y, z, c))

    def relay(j, rel):
        for n, d in enumerate((1, 3)):
            rcopy(kvout.at[0], kv_all.at[j, (d * 2 + rel) * TOK:(d * 2 + rel + 1) * TOK],
                  ag_ss.at[0, n], ag_rs.at[j, n, rel], dev(xp, y, z, c)).wait_recv()
            cp = relay_copy(j, rel, n)
            cp.start()
            sends.append(cp)

    def gathered(j):
        rcopy(kvout.at[0], kv_all.at[j, TOK:2 * TOK],
              ag_ss.at[0, 2], ag_rs.at[j, 2, 1], dev(x, y, z, 1 - c)).wait_recv()
        for rel in range(2):
            for n in range(2):
                relay_copy(j, rel, n).wait_recv()

    ZR = 2 * ROWS

    def block_rows(b):
        return pl.ds(pl.multiple_of(b * ZR, ZR), ZR)

    def product(j, first, count):
        def one(i, _):
            r = block_rows((z + first + i) % NZ)
            dw[j, r, :] = jnp.dot(xt_all[r, :], kv_all[j], preferred_element_type=F32)
            return 0

        lax.fori_loop(0, count, one, 0)

    def z_copy(j, way, step, sub):
        cols_ = slice(sub * HD, (sub + 1) * HD)
        return rcopy(zsend.at[j, way, step - 1, :, cols_], zrecv.at[j, way, step - 1, :, cols_],
                     z_ss.at[j, way, step - 1, sub], z_rs.at[j, way, step - 1, sub],
                     dev(x, y, zp if way == 0 else zm, c))

    def z_step(j, step):
        for sub in range(2):
            for way in range(2):
                if step == 1 and sub != way:
                    continue
                off = 5 - step if way == 0 else 3 + step
                r = block_rows((z + off) % NZ)
                cols_ = slice(sub * HD, (sub + 1) * HD)
                value = dw[j, r, cols_]
                if step > 2 or (step == 2 and sub == way):
                    z_copy(j, way, step - 1, sub).wait_recv()
                    value = value + zrecv[j, way, step - 2, :, cols_].astype(F32)
                zsend[j, way, step - 1, :, cols_] = value.astype(BF16)
                cp = z_copy(j, way, step, sub)
                cp.start()
                sends.append(cp)

    def y_copy(j, t):
        target = t * 2 + j
        slot = (y - target + 4) % NY - 1
        return rcopy(ysend.at[j, t], yrecv.at[slot], y_ss.at[j, t], y_rs.at[slot],
                     dev(x, target, z, c))

    def z_end(j):
        r = block_rows(z)
        for sub in range(2):
            cols_ = slice(sub * HD, (sub + 1) * HD)
            value = dw[j, r, cols_]
            for way in range(2):
                z_copy(j, way, 4, sub).wait_recv()
                value = value + zrecv[j, way, 3, :, cols_].astype(F32)
            dw[j, r, cols_] = value
            for t in range(2):
                ysend[j, t, :, cols_] = value[t * ROWS:(t + 1) * ROWS].astype(BF16)
        for t in range(2):
            @pl.when(y != t * 2 + j)
            def _(t=t):
                y_copy(j, t).start()

    def y_end(j):
        @pl.when(yl == j)
        def _():
            r = pl.ds(pl.multiple_of(z * ZR + yh * ROWS, ROWS), ROWS)
            total = dw[j, r, :]
            for slot in range(3):
                rcopy(ysend.at[j, 0], yrecv.at[slot], y_ss.at[j, 0], y_rs.at[slot],
                      dev(x, (y + 2) % NY, z, c)).wait_recv()
                total = total + yrecv[slot].astype(F32)
            total = total * (1.0 / 64.0)
            wk_ref[...] = total[:, 0:HD]
            wv_ref[...] = total[:, HD:2 * HD]

    attention(0)
    attention(1)
    finalize(0)
    attention(2)
    finalize(1)
    for d in (1, 3, 2):
        rcopy(xt_send.at[d - 1], xt_slot(xt_all, d, 0), x_ss.at[d - 1], x_rs.at[d - 1],
              dev((x + d) % NX, y, z, c)).wait_recv()
        x_forward(d)
    relay(0, 0)
    relay(0, 1)
    attention(3)
    finalize(2)
    for d in range(4):
        rcopy(xt_slot(xt_all, d, 0), xt_slot(xt_all, d, 1), xf_ss.at[d], xf_rs.at[d],
              dev(x, y, z, 1 - c)).wait_recv()
    gathered(0)
    product(0, 4, 1)
    z_step(0, 1)
    product(0, 5, 7)
    z_step(0, 2)
    finalize(3)
    z_step(0, 3)
    relay(1, 0)
    relay(1, 1)
    z_step(0, 4)
    gathered(1)
    product(1, 4, 1)
    z_step(1, 1)
    product(1, 5, 7)
    z_end(0)
    for step in (2, 3, 4):
        z_step(1, step)
    y_end(0)
    z_end(1)
    y_end(1)

    for cp in sends:
        cp.wait_send()
    for h in range(KVH):
        @pl.when((c + h) % 2 == 1)
        def _(h=h):
            rcopy(kvout.at[h], kv_all.at[h // 2, TOK:2 * TOK],
                  ag_ss.at[h, 2], ag_rs.at[h // 2, 2, 1], dev(x, y, z, 1 - c)).wait_send()
    for j in range(2):
        for t in range(2):
            @pl.when(y != t * 2 + j)
            def _(j=j, t=t):
                y_copy(j, t).wait_send()
    for cp in out_copies:
        cp.wait()


def per_device(layer_input, query_states, key_states, value_states, output_grads, doc_lengths):
    any_spec = pl.BlockSpec(memory_space=pl.ANY)
    vmem = pl.BlockSpec(memory_space=pltpu.VMEM)
    dma = pltpu.SemaphoreType.DMA
    dq, wk, wv = pl.pallas_call(
        kernel,
        out_shape=(
            jax.ShapeDtypeStruct((TOK, KVH * GROUP * HD), BF16),
            jax.ShapeDtypeStruct((ROWS, HD), F32),
            jax.ShapeDtypeStruct((ROWS, HD), F32),
        ),
        in_specs=[pl.BlockSpec(memory_space=pltpu.SMEM)] + [any_spec] * 5,
        out_specs=(any_spec, vmem, vmem),
        scratch_shapes=[
            pltpu.VMEM((TOK, D), BF16),
            pltpu.VMEM((TOK, KVH * GROUP * HD), BF16),
            pltpu.VMEM((TOK, KVH * GROUP * HD), BF16),
            pltpu.VMEM((KVH, 2, 3 * TOK, HD), BF16),
            pltpu.VMEM((TOK, 3 * TOK), F32),
            pltpu.VMEM((GROUP * TOK, 3 * TOK), BF16),
            pltpu.VMEM((GROUP * TOK, 3 * TOK), BF16),
            pltpu.VMEM((TOK, KVH * GROUP * HD), BF16),
            pltpu.VMEM((3, XW, TOK), BF16),
            pltpu.VMEM((XW, 8 * TOK), BF16),
            pltpu.VMEM((KVH, 2, HD, TOK), F32),
            pltpu.VMEM((KVH, 2, 2, HD, TOK), BF16),
            pltpu.VMEM((KVH, 2, 2, HD, TOK), BF16),
            pltpu.VMEM((KVH, TOK, 2 * HD), BF16),
            pltpu.VMEM((2, 8 * TOK, 2 * HD), BF16),
            pltpu.VMEM((2, XW, 2 * HD), F32),
            pltpu.VMEM((2, 2, 4, 2 * ROWS, 2 * HD), BF16),
            pltpu.VMEM((2, 2, 4, 2 * ROWS, 2 * HD), BF16),
            pltpu.VMEM((2, 2, ROWS, 2 * HD), BF16),
            pltpu.VMEM((3, ROWS, 2 * HD), BF16),
            dma((11,)),
            dma((KVH, 2)), dma((KVH, 2)),
            dma((3,)), dma((3,)),
            dma((4,)), dma((4,)),
            dma((KVH, 2)), dma((KVH, 2)),
            dma((KVH, 3)), dma((2, 3, 2)),
            dma((2, 2, 2)), dma((2, 2, 2)),
            dma((2, 2, 4, 2)), dma((2, 2, 4, 2)),
            dma((2, 2)), dma((3,)),
            dma((KVH,)),
        ],
        compiler_params=pltpu.CompilerParams(
            collective_id=0, has_side_effects=True, vmem_limit_bytes=40 * 1024 * 1024,
        ),
        cost_estimate=pl.CostEstimate(
            flops=2_600_000_000, bytes_accessed=4_000_000, transcendentals=1_000_000),
    )(doc_lengths, layer_input[0], query_states[0], key_states[0], value_states[0],
      output_grads[0])
    return dq[None], wk, wv


def solution(mesh):
    return jax.shard_map(
        per_device,
        mesh=mesh,
        in_specs=(
            P("dp", "seq", None),
            P("dp", "seq", None),
            P("dp", "seq", None),
            P("dp", "seq", None),
            P("dp", "seq", None),
            P("dp", None),
        ),
        out_specs=(P("dp", "seq", None), P("dp", "seq"), P("dp", "seq")),
        check_vma=False,
    )
```

time: 611 us -> 72.7 us (0.12)
  the two profiles are of different devices: /device:TPU:9 before, /device:TPU:8 now
where the time goes in v1:
time: 72.7 us; the launch traced here: 72.5 us
  Pallas kernels  63.8 us (88%)
  local copies, waits for them, and re-layouts  8.02 us (11%)
    pallas_call x1, Pallas kernels, per_device(): pl.pallas_call(kernel, out_shape=(jax.ShapeDtypeStruct((TOK, KVH * GROUP...  63.8 us
    unnamed x15, local copies, waits for them, and re-layouts  8.02 us

profile of v1, /device:TPU:8, one launch (start us, length us, event | category | flops | bytes accessed | tf_op | source)
XLA Modules:
  0.0 72.5 jit_solution(16399505764496650443)
XLA Ops:
  0.6 0.0 copy-start
  0.6 1.3 %copy-done = bf16[1,128,5120]{2,1,0:T(8,128)(2,1)S(1)} copy-done((bf16[1,128,5120]{2,1,0:T(8,128)(2,1)S(1)}, bf16[1,128,5120]{2,1,0:T(8,128)(2,1)}, u32[]{:S(2)}) %copy-start) | copy-done | bytes 1310744
  1.9 0.0 copy-start.1
  2.0 1.1 %copy-done.1 = bf16[1,128,2560]{2,1,0:T(8,128)(2,1)S(1)} copy-done((bf16[1,128,2560]{2,1,0:T(8,128)(2,1)S(1)}, bf16[1,128,2560]{2,1,0:T(8,128)(2,1)}, u32[]{:S(2)}) %copy-start.1) | copy-done | bytes 655384
  3.0 0.0 copy-start.2
  3.0 1.1 %copy-done.2 = bf16[1,128,2560]{2,1,0:T(8,128)(2,1)S(1)} copy-done((bf16[1,128,2560]{2,1,0:T(8,128)(2,1)S(1)}, bf16[1,128,2560]{2,1,0:T(8,128)(2,1)}, u32[]{:S(2)}) %copy-start.2) | copy-done | bytes 655384
  4.1 0.0 copy-start.3
  4.1 0.9 %copy-done.3 = bf16[1,128,512]{2,1,0:T(8,128)(2,1)S(1)} copy-done((bf16[1,128,512]{2,1,0:T(8,128)(2,1)S(1)}, bf16[1,128,512]{2,1,0:T(8,128)(2,1)}, u32[]{:S(2)}) %copy-start.3) | copy-done | bytes 131096
  5.0 0.0 copy-start.4
  5.0 0.9 %copy-done.4 = bf16[1,128,512]{2,1,0:T(8,128)(2,1)S(1)} copy-done((bf16[1,128,512]{2,1,0:T(8,128)(2,1)S(1)}, bf16[1,128,512]{2,1,0:T(8,128)(2,1)}, u32[]{:S(2)}) %copy-start.4) | copy-done | bytes 131096
  5.9 0.0 copy-start.5
  5.9 0.7 copy-done.5
  6.6 63.8 %shard_map.85 = (bf16[128,2560]{1,0:T(8,128)(2,1)S(1)}, f32[80,128]{1,0:T(8,128)S(1)}, f32[80,128]{1,0:T(8,128)S(1)}) custom-call(s32[1,6]{1,0:T(1,128)S(1)} %copy-done.5, bf16[128,5120]{1,0:T(8,128)(2,1)S(1)} %bitcast.7, bf16[128,2560]{1,0:T(8,128)(2,1)S(1)} %bitcast.8, bf16[128,512]{1,0:T(8,128)(2,1)S(1)} %bitcast.10, bf16[128,512]{1,0:T(8,128)(2,1)S(1)} %bitcast.11, ...), custom_call_target="tpu_custom_call" | custom-call | flops 2600000000 | bytes 4000000 | tf_op jit(solution)/shard_map/pallas_call | solution.py:366
  70.4 0.8 %copy.12 = bf16[1,128,2560]{2,1,0:T(8,128)(2,1)} copy(bf16[1,128,2560]{2,1,0:T(8,128)(2,1)S(1)} %bitcast.6) | data formatting | bytes 1310720
  71.2 0.6 copy.13
  71.8 0.6 copy.14
Async XLA Ops:
  0.6 1.3 %copy-start = (bf16[1,128,5120]{2,1,0:T(8,128)(2,1)S(1)}, bf16[1,128,5120]{2,1,0:T(8,128)(2,1)}, u32[]{:S(2)}) copy-start(bf16[1,128,5120]{2,1,0:T(8,128)(2,1)} %param.6) | copy-start | bytes 3932164
  1.9 1.1 %copy-start.1 = (bf16[1,128,2560]{2,1,0:T(8,128)(2,1)S(1)}, bf16[1,128,2560]{2,1,0:T(8,128)(2,1)}, u32[]{:S(2)}) copy-start(bf16[1,128,2560]{2,1,0:T(8,128)(2,1)} %param.7) | copy-start | bytes 1966084
  3.0 1.1 %copy-start.2 = (bf16[1,128,2560]{2,1,0:T(8,128)(2,1)S(1)}, bf16[1,128,2560]{2,1,0:T(8,128)(2,1)}, u32[]{:S(2)}) copy-start(bf16[1,128,2560]{2,1,0:T(8,128)(2,1)} %param.10) | copy-start | bytes 1966084
  4.1 0.9 %copy-start.3 = (bf16[1,128,512]{2,1,0:T(8,128)(2,1)S(1)}, bf16[1,128,512]{2,1,0:T(8,128)(2,1)}, u32[]{:S(2)}) copy-start(bf16[1,128,512]{2,1,0:T(8,128)(2,1)} %param.8) | copy-start | bytes 393220
  5.0 0.9 %copy-start.4 = (bf16[1,128,512]{2,1,0:T(8,128)(2,1)S(1)}, bf16[1,128,512]{2,1,0:T(8,128)(2,1)}, u32[]{:S(2)}) copy-start(bf16[1,128,512]{2,1,0:T(8,128)(2,1)} %param.9) | copy-start | bytes 393220
  5.9 0.7 copy-start.5

commit v2 on v1

v2 whole, which is shorter than its diff:
```python
import jax
import jax.numpy as jnp
from jax import lax
from jax.experimental import pallas as pl
from jax.experimental.pallas import tpu as pltpu
from jax.sharding import PartitionSpec as P

HD = 128
KVH = 4
GROUP = 5
TOK = 128
D = 5120
XW = D // 4
NX, NY, NZ = 4, 4, 8
ROWS = 80
LOG2E = 1.4426950408889634
SCALE = HD ** (-0.5)
MESH = pl.DeviceIdType.MESH
F32 = jnp.float32
BF16 = jnp.bfloat16


def kernel(
    doc_ref, x_hbm, q_hbm, k_hbm, v_hbm, do_hbm,
    dq_ref, wk_ref, wv_ref,
    xin, qin, doin, kv, bias, ds_s, pb_s, xt_send, xt_all,
    part_own, part_send, part_recv, kvout, kv_all, dw, a_send, a_recv, b_send, b_recv,
    fa_send, fb_send, fa, fb,
    ld_sem, kv_ss, kv_rs, x_ss, x_rs, xl_sem, xf_ss, xf_rs, p_ss, p_rs,
    ag_ss, ag_rs, a_ss, a_rs, b_ss, b_rs, fa_ss, fa_rs, fb_ss, fb_rs,
):
    dp = lax.axis_index("dp")
    sq = lax.axis_index("seq")
    x = dp // 16
    z = (dp // 2) % 8
    yh = dp % 2
    yl = sq // 2
    c = sq % 2
    y = yh * 2 + yl

    def dev(xx, yy, zz, cc):
        return ((xx * 8 + zz) * 2 + yy // 2, (yy % 2) * 2 + cc)

    def seq_dev(delta):
        return (dp, (sq + delta) % 4)

    sibling = dev(x, y, z, 1 - c)

    def rcopy(src, dst, ss, rs, device):
        return pltpu.make_async_remote_copy(
            src_ref=src, dst_ref=dst, send_sem=ss, recv_sem=rs,
            device_id=device, device_id_type=MESH,
        )

    load_x = pltpu.make_async_copy(x_hbm, xin, ld_sem.at[8])
    load_q = pltpu.make_async_copy(q_hbm, qin, ld_sem.at[9])
    load_do = pltpu.make_async_copy(do_hbm, doin, ld_sem.at[10])
    loads = []
    for h in range(KVH):
        for i, ref in enumerate((k_hbm, v_hbm)):
            loads.append(pltpu.make_async_copy(
                ref.at[:, h * HD:(h + 1) * HD], kv.at[h, i, 256:384], ld_sem.at[h * 2 + i]))
    load_x.start()
    for cp in loads:
        cp.start()
    load_q.start()
    load_do.start()

    barrier = pltpu.get_barrier_semaphore()
    out_y = (y + 3 + 2 * yl) % NY
    peers = [dev(x, y, (z + d) % NZ, cc) for d in (4, 3, 5, 2, 6, 1, 7) for cc in (c, 1 - c)]
    peers += [dev((x + d) % NX, y, z, cc) for d in (2, 1, 3) for cc in (c, 1 - c)]
    peers += [dev(x, yy, z, cc) for yy in ((y + 2) % NY, out_y) for cc in (c, 1 - c)]
    peers += [seq_dev(1), seq_dev(2), seq_dev(3)]
    for peer in peers:
        pl.semaphore_signal(barrier, inc=1, device_id=peer, device_id_type=MESH)

    def turn_block(d):
        target = (x + d) % NX

        def turn(i, _):
            col = pl.multiple_of(target * XW + i * 128, 128)
            row = pl.multiple_of(i * 128, 128)
            xt_send[d, pl.ds(row, 128), :] = xin[:, pl.ds(col, 128)].T
            return 0

        lax.fori_loop(0, XW // 128, turn, 0)

    def x_slot(d, rel, t):
        return xt_all.at[t, :, :, (d * 2 + rel) * TOK:(d * 2 + rel + 1) * TOK]

    def x_copy(d, t):
        src = xt_send.at[d].reshape(NZ, 2, ROWS, TOK).at[:, t]
        if d == 0:
            return pltpu.make_async_copy(src, x_slot(0, 0, t), xl_sem.at[t])
        return rcopy(src, x_slot(d, 0, t), x_ss.at[d - 1, t], x_rs.at[d - 1, t],
                     dev((x + d) % NX, y, z, c))

    def x_forward(d, t):
        return rcopy(x_slot(d, 0, t), x_slot(d, 1, t), xf_ss.at[d, t], xf_rs.at[d, t], sibling)

    sends = []

    def start(cp):
        cp.start()
        sends.append(cp)

    load_x.wait()
    turn_block(2)

    for cp in loads:
        cp.wait()
    pl.semaphore_wait(barrier, len(peers))

    def kv_copy(h, delta):
        return rcopy(kv.at[h, :, 256:384], kv.at[h, :, (2 - delta) * TOK:(3 - delta) * TOK],
                     kv_ss.at[h, delta - 1], kv_rs.at[h, delta - 1], seq_dev(delta))

    for h in range(KVH):
        for delta in (2, 1):
            start(kv_copy(h, delta))
    for d in (2, 1, 3, 0):
        if d != 2:
            turn_block(d)
        for t in range(2):
            if d == 0:
                x_copy(0, t).start()
            else:
                start(x_copy(d, t))

    rows = lax.broadcasted_iota(jnp.int32, (TOK, 1), 0) + sq * TOK
    first = jnp.zeros((TOK, 1), jnp.int32)
    end = jnp.int32(0)
    for n in range(6):
        end = end + doc_ref[0, n]
        first = jnp.where(rows >= end, end, first)
    cols = lax.broadcasted_iota(jnp.int32, (TOK, 384), 1) + (sq - 2) * TOK
    bias[...] = jnp.where((cols >= first) & (cols <= rows), 0.0, -1e30).astype(F32)

    load_q.wait()
    load_do.wait()

    def part_copy(h, delta):
        return rcopy(part_send.at[h, delta - 1], part_recv.at[h, delta - 1],
                     p_ss.at[h, delta - 1], p_rs.at[h, delta - 1], seq_dev(4 - delta))

    def attention(h):
        for delta in (1, 2):
            kv_copy(h, delta).wait_recv()
        for g in range(GROUP):
            at = slice((h * GROUP + g) * HD, (h * GROUP + g + 1) * HD)
            to = slice(g * TOK, (g + 1) * TOK)
            kk = kv[h, 0]
            s = lax.dot_general(qin[:, at], kk, (((1,), (1,)), ((), ())),
                                preferred_element_type=F32)
            s = s * (SCALE * LOG2E) + bias[...]
            m = jnp.max(s, axis=1, keepdims=True)
            e = jnp.exp2(s - m)
            p = e * (1.0 / jnp.sum(e, axis=1, keepdims=True))
            dpr = lax.dot_general(doin[:, at], kv[h, 1], (((1,), (1,)), ((), ())),
                                  preferred_element_type=F32)
            delta_r = jnp.sum(p * dpr, axis=1, keepdims=True)
            ds = (p * (dpr - delta_r) * SCALE).astype(BF16)
            ds_s[to, :] = ds
            pb_s[to, :] = p.astype(BF16)
            dq_ref[:, at] = jnp.dot(ds, kk, preferred_element_type=F32).astype(BF16)
        for i, (src, grads) in enumerate(((qin, ds_s), (doin, pb_s))):
            stacked = jnp.concatenate(
                [src[:, (h * GROUP + g) * HD:(h * GROUP + g + 1) * HD] for g in range(GROUP)],
                axis=0)
            t = lax.dot_general(stacked, grads[...], (((0,), (0,)), ((), ())),
                                preferred_element_type=F32)
            part_own[h, i] = t[:, 256:384]
            part_send[h, 0, i] = t[:, 128:256].astype(BF16)
            part_send[h, 1, i] = t[:, 0:128].astype(BF16)
        for delta in (2, 1):
            start(part_copy(h, delta))

    def ag_copy(h, i, d):
        rel = (c + i) % 2
        rows_ = pl.ds(pl.multiple_of((d * 2 + rel) * TOK, TOK), TOK)
        return rcopy(kvout.at[h, i], kv_all.at[h, rows_], ag_ss.at[h, i, d - 1],
                     ag_rs.at[h, d, rel], dev((x + d) % NX, y, z, i))

    def ag_sibling(h):
        return rcopy(kvout.at[h, 1 - c], kv_all.at[h, TOK:2 * TOK],
                     ag_ss.at[h, 0, 3], ag_rs.at[h, 0, 1], sibling)

    def finalize(h):
        for delta in (1, 2):
            part_copy(h, delta).wait_recv()
        for i in range(2):
            total = (part_own[h, i] + part_recv[h, 0, i].astype(F32)
                     + part_recv[h, 1, i].astype(F32))
            kvout[h, i] = total.T.astype(BF16)
        for d in (2, 1, 3):
            for i in range(2):
                start(ag_copy(h, i, d))
        start(ag_sibling(h))
        kv_all[h, 0:TOK] = kvout[h, c]

    def gathered(h):
        ag_sibling(h).wait_recv()
        for d in (1, 3, 2):
            for rel in range(2):
                rcopy(kvout.at[h, 0], kv_all.at[h, (d * 2 + rel) * TOK:(d * 2 + rel + 1) * TOK],
                      ag_ss.at[h, 0, 0], ag_rs.at[h, d, rel], sibling).wait_recv()

    HALF = NZ * ROWS

    def product(h):
        for part in range(2):
            t = c if part == 0 else 1 - c
            for n in range(2):
                w = xt_all[t, n * 4:(n + 1) * 4].reshape(HALF // 2, 8 * TOK)
                out = jnp.dot(w, kv_all[h], preferred_element_type=F32)
                out = out.reshape(4, ROWS, HD)
                dw[h, part, n * 4:(n + 1) * 4] = out
                send = a_send if part == 0 else b_send
                send[h, n * 4:(n + 1) * 4] = out.astype(BF16)
            if part == 0:
                for d in (4, 3, 5, 2, 6, 1, 7):
                    start(a_copy(h, d))
            else:
                @pl.when(y != (1 - c) * 2 + h // 2)
                def _():
                    b_copy(h).start()

    def a_copy(h, d):
        target = (z + d) % NZ
        return rcopy(a_send.at[h, target], a_recv.at[h, d - 1], a_ss.at[h, d - 1],
                     a_rs.at[h, d - 1], dev(x, y, target, c))

    def b_copy(h):
        target = (1 - c) * 2 + h // 2
        slot = (y - target + 4) % NY - 1
        return rcopy(b_send.at[h], b_recv.at[h % 2, slot], b_ss.at[h], b_rs.at[h % 2, slot],
                     dev(x, target, z, c))

    def fa_copy(h):
        return rcopy(fa_send.at[h], fa.at[y], fa_ss.at[h], fa_rs.at[y],
                     dev(x, c * 2 + h // 2, z, h % 2))

    def fa_self(h):
        return (y == c * 2 + h // 2) & (c == h % 2)

    def fb_copy(h, target):
        return rcopy(fb_send.at[h % 2, target], fb.at[z], fb_ss.at[h % 2, target], fb_rs.at[z],
                     dev(x, y, target, h % 2))

    def b_owner(h):
        return y == (1 - c) * 2 + h // 2

    def spread(h):
        for d in range(1, NZ):
            a_copy(h, d).wait_recv()
        total = dw[h, 0, z]
        for d in range(1, NZ):
            total = total + a_recv[h, d - 1].astype(F32)
        total = total.astype(BF16)
        fa_send[h] = total

        @pl.when(fa_self(h))
        def _():
            fa[y] = total

        @pl.when(jnp.logical_not(fa_self(h)))
        def _():
            fa_copy(h).start()

        @pl.when(b_owner(h))
        def _():
            for slot in range(3):
                rcopy(b_send.at[h], b_recv.at[h % 2, slot], b_ss.at[h], b_rs.at[h % 2, slot],
                      dev(x, (y + 2) % NY, z, c)).wait_recv()
            t = dw[h, 1]
            for slot in range(3):
                t = t + b_recv[h % 2, slot].astype(F32)
            fb_send[h % 2] = t.astype(BF16)
            for d in (4, 3, 5, 2, 6, 1, 7):
                fb_copy(h, (z + d) % NZ).start()

            @pl.when(c != h % 2)
            def _():
                fb_copy(h, z).start()

            @pl.when(c == h % 2)
            def _():
                fb[z] = fb_send[h % 2, z]

    def finish():
        own_a = yh == c
        for s in range(NY):
            @pl.when(jnp.logical_not(own_a & (y == s)))
            def _(s=s):
                rcopy(fa_send.at[0], fa.at[s], fa_ss.at[0], fa_rs.at[s], sibling).wait_recv()
        for s in range(NZ):
            @pl.when(own_a | (z != s))
            def _(s=s):
                rcopy(fa_send.at[0], fb.at[s], fa_ss.at[0], fb_rs.at[s], sibling).wait_recv()
        ta = fa[0].astype(F32)
        for s in range(1, NY):
            ta = ta + fa[s].astype(F32)
        tb = fb[0].astype(F32)
        for s in range(1, NZ):
            tb = tb + fb[s].astype(F32)
        ta = ta * (1.0 / 64.0)
        tb = tb * (1.0 / 64.0)
        wk_ref[...] = jnp.where(yh == 0, ta, tb)
        wv_ref[...] = jnp.where(yh == 0, tb, ta)

    attention(0)
    start_x0 = [x_copy(0, t) for t in range(2)]
    for t in range(2):
        start_x0[t].wait()
        start(x_forward(0, t))
    attention(1)
    attention(2)
    finalize(0)
    attention(3)
    finalize(1)
    finalize(2)
    for d in (1, 3, 2):
        for t in range(2):
            x_copy(d, t).wait_recv()
            start(x_forward(d, t))
    finalize(3)
    for d in range(4):
        for t in range(2):
            x_forward(d, t).wait_recv()
    for h in range(KVH):
        gathered(h)
        product(h)
        if h > 0:
            spread(h - 1)
    spread(3)
    finish()

    for cp in sends:
        cp.wait_send()
    for h in range(KVH):
        @pl.when(jnp.logical_not(b_owner(h)))
        def _(h=h):
            b_copy(h).wait_send()

        @pl.when(jnp.logical_not(fa_self(h)))
        def _(h=h):
            fa_copy(h).wait_send()

        @pl.when(b_owner(h))
        def _(h=h):
            for d in range(1, NZ):
                fb_copy(h, (z + d) % NZ).wait_send()

            @pl.when(c != h % 2)
            def _():
                fb_copy(h, z).wait_send()


def per_device(layer_input, query_states, key_states, value_states, output_grads, doc_lengths):
    hbm = pl.BlockSpec(memory_space=pltpu.HBM)
    vmem = pl.BlockSpec(memory_space=pltpu.VMEM)
    dma = pltpu.SemaphoreType.DMA
    dq, wk, wv = pl.pallas_call(
        kernel,
        out_shape=(
            jax.ShapeDtypeStruct((TOK, KVH * GROUP * HD), BF16),
            jax.ShapeDtypeStruct((ROWS, HD), F32),
            jax.ShapeDtypeStruct((ROWS, HD), F32),
        ),
        in_specs=[pl.BlockSpec(memory_space=pltpu.SMEM)] + [hbm] * 5,
        out_specs=(vmem, vmem, vmem),
        scratch_shapes=[
            pltpu.VMEM((TOK, D), BF16),
            pltpu.VMEM((TOK, KVH * GROUP * HD), BF16),
            pltpu.VMEM((TOK, KVH * GROUP * HD), BF16),
            pltpu.VMEM((KVH, 2, 3 * TOK, HD), BF16),
            pltpu.VMEM((TOK, 3 * TOK), F32),
            pltpu.VMEM((GROUP * TOK, 3 * TOK), BF16),
            pltpu.VMEM((GROUP * TOK, 3 * TOK), BF16),
            pltpu.VMEM((4, XW, TOK), BF16),
            pltpu.VMEM((2, NZ, ROWS, 8 * TOK), BF16),
            pltpu.VMEM((KVH, 2, HD, TOK), F32),
            pltpu.VMEM((KVH, 2, 2, HD, TOK), BF16),
            pltpu.VMEM((KVH, 2, 2, HD, TOK), BF16),
            pltpu.VMEM((KVH, 2, TOK, HD), BF16),
            pltpu.VMEM((KVH, 8 * TOK, HD), BF16),
            pltpu.VMEM((KVH, 2, NZ, ROWS, HD), F32),
            pltpu.VMEM((KVH, NZ, ROWS, HD), BF16),
            pltpu.VMEM((KVH, NZ - 1, ROWS, HD), BF16),
            pltpu.VMEM((KVH, NZ, ROWS, HD), BF16),
            pltpu.VMEM((2, 3, NZ, ROWS, HD), BF16),
            pltpu.VMEM((KVH, ROWS, HD), BF16),
            pltpu.VMEM((2, NZ, ROWS, HD), BF16),
            pltpu.VMEM((NY, ROWS, HD), BF16),
            pltpu.VMEM((NZ, ROWS, HD), BF16),
            dma((11,)),
            dma((KVH, 2)), dma((KVH, 2)),
            dma((3, 2)), dma((3, 2)), dma((2,)),
            dma((4, 2)), dma((4, 2)),
            dma((KVH, 2)), dma((KVH, 2)),
            dma((KVH, 2, 4)), dma((KVH, 4, 2)),
            dma((KVH, NZ - 1)), dma((KVH, NZ - 1)),
            dma((KVH,)), dma((2, 3)),
            dma((KVH,)), dma((NY,)),
            dma((2, NZ)), dma((NZ,)),
        ],
        compiler_params=pltpu.CompilerParams(
            collective_id=0, has_side_effects=True, vmem_limit_bytes=40 * 1024 * 1024,
        ),
        cost_estimate=pl.CostEstimate(
            flops=2_600_000_000, bytes_accessed=4_000_000, transcendentals=1_000_000),
    )(pltpu.with_memory_space_constraint(doc_lengths, pltpu.HBM), *[pltpu.with_memory_space_constraint(a[0], pltpu.HBM) for a in (
        layer_input, query_states, key_states, value_states, output_grads)])
    return dq[None], wk, wv


def solution(mesh):
    return jax.shard_map(
        per_device,
        mesh=mesh,
        in_specs=(
            P("dp", "seq", None),
            P("dp", "seq", None),
            P("dp", "seq", None),
            P("dp", "seq", None),
            P("dp", "seq", None),
            P("dp", None),
        ),
        out_specs=(P("dp", "seq", None), P("dp", "seq"), P("dp", "seq")),
        check_vma=False,
    )
```

time: 72.7 us -> 57.7 us (0.79)
  the two profiles are of different devices: /device:TPU:8 before, /device:TPU:9 now
where the time goes in v2:
time: 57.7 us; the launch traced here: 57.6 us
  Pallas kernels  54.9 us (95%)
  local copies, waits for them, and re-layouts  2.07 us (4%)
  between operations  0.64 us (1%)
    pallas_call x1, Pallas kernels, per_device(): pl.pallas_call(kernel, out_shape=(jax.ShapeDtypeStruct((TOK, KVH * GROUP...  54.9 us
    unnamed x3, local copies, waits for them, and re-layouts  2.07 us

profile of v2, /device:TPU:9, one launch (start us, length us, event | category | flops | bytes accessed | tf_op | source)
XLA Modules:
  0.0 57.6 jit_solution(17649955105689481293)
XLA Ops:
  0.6 54.9 %shard_map.85 = (bf16[128,2560]{1,0:T(8,128)(2,1)S(1)}, f32[80,128]{1,0:T(8,128)S(1)}, f32[80,128]{1,0:T(8,128)S(1)}) custom-call(s32[1,6]{1,0:T(1,128)} %doc_ref.1, bf16[128,5120]{1,0:T(8,128)(2,1)} %bitcast.7, bf16[128,2560]{1,0:T(8,128)(2,1)} %bitcast.8, bf16[128,512]{1,0:T(8,128)(2,1)} %bitcast.10, bf16[128,512]{1,0:T(8,128)(2,1)} %bitcast.11, ...), custom_call_target="tpu_custom_call" | custom-call | flops 2600000000 | bytes 4000000 | tf_op jit(solution)/shard_map/pallas_call | solution.py:364
  55.5 0.8 %copy.12 = bf16[1,128,2560]{2,1,0:T(8,128)(2,1)} copy(bf16[1,128,2560]{2,1,0:T(8,128)(2,1)S(1)} %bitcast.6) | data formatting | bytes 1310720
  56.3 0.6 %copy.13 = f32[80,128]{1,0:T(8,128)} copy(f32[80,128]{1,0:T(8,128)S(1)} %get-tuple-element.13) | data formatting | bytes 81920
  57.0 0.6 %copy.14 = f32[80,128]{1,0:T(8,128)} copy(f32[80,128]{1,0:T(8,128)S(1)} %get-tuple-element.14) | data formatting | bytes 81920

commit v3 on v2

v3 whole, which is shorter than its diff:
```python
import jax
import jax.numpy as jnp
from jax import lax
from jax.experimental import pallas as pl
from jax.experimental.pallas import tpu as pltpu
from jax.sharding import PartitionSpec as P

HD = 128
KVH = 4
GROUP = 5
TOK = 128
D = 5120
XW = D // 4
NX, NY, NZ = 4, 4, 8
ROWS = 80
LOG2E = 1.4426950408889634
SCALE = HD ** (-0.5)
MESH = pl.DeviceIdType.MESH
F32 = jnp.float32
BF16 = jnp.bfloat16


def kernel(
    doc_ref, x_hbm, q_hbm, k_hbm, v_hbm, do_hbm,
    dq_ref, wk_ref, wv_ref,
    xin, qin, doin, kv, bias, xt_send, xt_all,
    part_own, part_send, part_recv, kvout, kv_all, a_send, a_recv, b_send, b_recv,
    fa_send, fb_send, fa, fb,
    ld_sem, kv_ss, kv_rs, x_ss, x_rs, xl_sem, xf_ss, xf_rs, p_ss, p_rs,
    ag_ss, ag_rs, a_ss, a_rs, b_ss, b_rs, fa_ss, fa_rs, fb_ss, fb_rs,
):
    dp = lax.axis_index("dp")
    sq = lax.axis_index("seq")
    div, rem = lax.div, lax.rem
    x, z, yh = div(dp, 16), rem(div(dp, 2), 8), rem(dp, 2)
    yl, c = div(sq, 2), rem(sq, 2)
    y = yh * 2 + yl
    xl, xh, zl, zh = rem(x, 2), div(x, 2), rem(z, 2), div(z, 2)
    x_next = (x + 1 - 2 * xl, rem(x + 3 + 2 * xl, NX))
    z_next = (z + 1 - 2 * zl, rem(z + 7 + 2 * zl, NZ))
    x_two = rem(x + 2, NX)
    zh_on = [zh] + [rem(zh + k, 4) for k in (1, 2, 3)]
    z_on = [zl + 2 * k for k in zh_on]
    ranks = [sq] + [rem(sq + k, 4) for k in (1, 2, 3)]
    here, over, across, beyond = (yh, yl), (1 - yh, yl), (yh, 1 - yl), (1 - yh, 1 - yl)

    def member(t, m):
        return (x_next[t] if m // 2 else x), (z_next[t] if m % 2 else z)

    def dev(xx, yy, zz, cc):
        return (xx * 16 + zz * 2 + yy[0], yy[1] * 2 + cc)

    def seq_dev(delta):
        return (dp, ranks[delta])

    sibling = dev(x, here, z, 1 - c)

    def rcopy(src, dst, ss, rs, device):
        return pltpu.make_async_remote_copy(
            src_ref=src, dst_ref=dst, send_sem=ss, recv_sem=rs,
            device_id=device, device_id_type=MESH,
        )

    load_x = pltpu.make_async_copy(x_hbm, xin, ld_sem.at[8])
    load_q = pltpu.make_async_copy(q_hbm, qin, ld_sem.at[9])
    load_do = pltpu.make_async_copy(do_hbm, doin, ld_sem.at[10])
    loads = []
    for h in range(KVH):
        for i, ref in enumerate((k_hbm, v_hbm)):
            loads.append(pltpu.make_async_copy(
                ref.at[:, h * HD:(h + 1) * HD], kv.at[h, i, 256:384], ld_sem.at[h * 2 + i]))
    load_x.start()
    for cp in loads:
        cp.start()
    load_q.start()
    load_do.start()

    barrier = pltpu.get_barrier_semaphore()
    peers = [seq_dev(1), seq_dev(2), seq_dev(3)]
    for t in range(2):
        for m in (3, 2, 1):
            xx, zz = member(t, m)
            peers += [dev(xx, here, zz, c), dev(xx, here, zz, 1 - c)]
    for k in (2, 1, 3, 0):
        zz = z_on[k]
        places = [(x_two, here), (x, over), (x, beyond)]
        if k > 0:
            places += [(x, here), (x, across)]
        for xx, yy in places:
            peers += [dev(xx, yy, zz, c), dev(xx, yy, zz, 1 - c)]
    for peer in peers:
        pl.semaphore_signal(barrier, inc=1, device_id=peer, device_id_type=MESH)

    def turn_block(xd):
        def turn(i, _):
            at = pl.multiple_of(xd * XW + i * 128, 128)
            xt_send[pl.ds(at, 128), :] = xin[:, pl.ds(at, 128)].T
            return 0

        lax.fori_loop(0, XW // 128, turn, 0)

    def x_copy(t, m):
        xx, zz = member(t, m)
        xo, zo = (1 - xl if m // 2 else xl), (1 - zl if m % 2 else zl)
        src = xt_send.reshape(2, 2, 4, 2, 2, ROWS, TOK).at[:, xo, :, zo, t]
        if m == 0:
            return pltpu.make_async_copy(src, xt_all.at[t, 0], xl_sem.at[t])
        return rcopy(src, xt_all.at[t, m * 2], x_ss.at[t, m - 1], x_rs.at[t, m - 1],
                     dev(xx, here, zz, c))

    def x_forward(t, m):
        return rcopy(xt_all.at[t, m * 2], xt_all.at[t, m * 2 + 1], xf_ss.at[t, m], xf_rs.at[t, m],
                     sibling)

    sends = []

    def start(cp):
        cp.start()
        sends.append(cp)

    for cp in loads:
        cp.wait()
    pl.semaphore_wait(barrier, len(peers))

    def kv_copy(h, delta):
        return rcopy(kv.at[h, :, 256:384], kv.at[h, :, (2 - delta) * TOK:(3 - delta) * TOK],
                     kv_ss.at[h, delta - 1], kv_rs.at[h, delta - 1], seq_dev(delta))

    for h in range(KVH):
        for delta in (2, 1):
            @pl.when(sq + delta < 4)
            def _(h=h, delta=delta):
                kv_copy(h, delta).start()
    for delta in (1, 2):
        @pl.when(sq < delta)
        def _(delta=delta):
            kv[:, :, (2 - delta) * TOK:(3 - delta) * TOK] = jnp.zeros((KVH, 2, TOK, HD), BF16)

        @pl.when(sq + delta > 3)
        def _(delta=delta):
            part_recv[:, delta - 1] = jnp.zeros((KVH, 2, HD, TOK), BF16)
    load_x.wait()
    for part in (1, 0):
        for half in range(2):
            turn_block((1 - xl if part else xl) + 2 * half)
        for t in range(2):
            if part:
                start(x_copy(t, 3))
                start(x_copy(t, 2))
            else:
                start(x_copy(t, 1))
                x_copy(t, 0).start()

    rows = lax.broadcasted_iota(jnp.int32, (TOK, 1), 0) + sq * TOK
    first = jnp.zeros((TOK, 1), jnp.int32)
    end = jnp.int32(0)
    for n in range(6):
        end = end + doc_ref[0, n]
        first = jnp.where(rows >= end, end, first)
    cols = lax.broadcasted_iota(jnp.int32, (TOK, 384), 1) + (sq - 2) * TOK
    bias[...] = jnp.where((cols >= first) & (cols <= rows), 0.0, -1e30).astype(F32)

    load_q.wait()
    load_do.wait()

    def part_copy(h, delta):
        return rcopy(part_send.at[h, delta - 1], part_recv.at[h, delta - 1],
                     p_ss.at[h, delta - 1], p_rs.at[h, delta - 1], seq_dev(4 - delta))

    def attention(h):
        for delta in (1, 2):
            @pl.when(sq >= delta)
            def _(delta=delta):
                kv_copy(h, delta).wait_recv()
        def stack(ref):
            return jnp.concatenate(
                [ref[:, (h * GROUP + g) * HD:(h * GROUP + g + 1) * HD] for g in range(GROUP)],
                axis=0)

        qs, dos = stack(qin), stack(doin)
        kk = kv[h, 0]
        nt = (((1,), (1,)), ((), ()))
        s = lax.dot_general(qs, kk, nt, preferred_element_type=F32).reshape(GROUP, TOK, 3 * TOK)
        dpr = lax.dot_general(dos, kv[h, 1], nt, preferred_element_type=F32)
        dpr = dpr.reshape(GROUP, TOK, 3 * TOK)
        s = s * (SCALE * LOG2E) + bias[...][None]
        m = jnp.max(s, axis=2, keepdims=True)
        e = jnp.exp2(s - m)
        p = e * (1.0 / jnp.sum(e, axis=2, keepdims=True))
        delta_r = jnp.sum(p * dpr, axis=2, keepdims=True)
        ds = (p * (dpr - delta_r) * SCALE).astype(BF16).reshape(GROUP * TOK, 3 * TOK)
        pb = p.astype(BF16).reshape(GROUP * TOK, 3 * TOK)
        tn = (((0,), (0,)), ((), ()))
        for i, (rows_in, grads) in enumerate(((qs, ds), (dos, pb))):
            t = lax.dot_general(rows_in, grads, tn, preferred_element_type=F32)
            part_own[h, i] = t[:, 256:384]
            part_send[h, 0, i] = t[:, 128:256].astype(BF16)
            part_send[h, 1, i] = t[:, 0:128].astype(BF16)
        for delta in (2, 1):
            @pl.when(sq >= delta)
            def _(delta=delta):
                part_copy(h, delta).start()
        dq = jnp.dot(ds, kk, preferred_element_type=F32).astype(BF16)
        for g in range(GROUP):
            dq_ref[:, (h * GROUP + g) * HD:(h * GROUP + g + 1) * HD] = dq[g * TOK:(g + 1) * TOK]

    def ag_copy(h, i, t, m):
        rel = 1 - c if i else c
        rows_ = pl.ds(pl.multiple_of((m * 2 + rel) * TOK, TOK), TOK)
        xx, zz = member(t, m)
        return rcopy(kvout.at[h, i], kv_all.at[t, h, rows_], ag_ss.at[h, i, t, m],
                     ag_rs.at[h, t, m, rel], dev(xx, here, zz, i))

    def ag_sibling(h, t):
        return rcopy(kvout.at[h, 1 - c], kv_all.at[t, h, TOK:2 * TOK],
                     ag_ss.at[h, 0, t, 0], ag_rs.at[h, t, 0, 1], sibling)

    def finalize(h):
        for delta in (1, 2):
            @pl.when(sq + delta < 4)
            def _(delta=delta):
                part_copy(h, delta).wait_recv()
        for i in range(2):
            total = (part_own[h, i] + part_recv[h, 0, i].astype(F32)
                     + part_recv[h, 1, i].astype(F32))
            kvout[h, i] = total.T.astype(BF16)
        for m in (3, 2, 1):
            for t in range(2):
                for i in range(2):
                    start(ag_copy(h, i, t, m))
        for t in range(2):
            start(ag_sibling(h, t))
            kv_all[t, h, 0:TOK] = kvout[h, c]

    def gathered(h):
        for t in range(2):
            ag_sibling(h, t).wait_recv()
            for m in (1, 2, 3):
                for rel in range(2):
                    rcopy(kvout.at[h, 0], kv_all.at[t, h, 0:TOK], ag_ss.at[h, 0, 0, 0],
                          ag_rs.at[h, t, m, rel], sibling).wait_recv()

    HALF = 8 * ROWS

    def product(h):
        for part in range(2):
            t = c if part == 0 else 1 - c
            send = a_send if part == 0 else b_send
            for n in range(2):
                w = jnp.concatenate(
                    [xt_all[t, s, n].reshape(4 * ROWS, TOK) for s in range(8)],
                    axis=1)
                out = jnp.dot(w, kv_all[t, h], preferred_element_type=F32)
                send[h, n * 4:(n + 1) * 4] = out.reshape(4, ROWS, HD).astype(BF16)
            if part == 0:
                start(a_copy(h))
            else:
                @pl.when(y != (1 - c) * 2 + h // 2)
                def _():
                    b_copy(h).start()

    def a_copy(h):
        src = a_send.reshape(KVH, 2, 4, ROWS, HD).at[h, 1 - xh]
        return rcopy(src, a_recv.at[h], a_ss.at[h], a_rs.at[h], dev(x_two, here, z, c))

    def b_copy(h):
        target = (1 - c) * 2 + h // 2
        slot = rem(y - target + 4, NY) - 1
        return rcopy(b_send.at[h], b_recv.at[h % 2, slot], b_ss.at[h], b_rs.at[h % 2, slot],
                     dev(x, (1 - c, h // 2), z, c))

    def fa_copy(h, k):
        return rcopy(fa_send.at[h, k], fa.at[y * 4 + zh], fa_ss.at[h, k], fa_rs.at[y * 4 + zh],
                     dev(x, (c, h // 2), zl + 2 * k, h % 2))

    def fa_self(h, k):
        return (y == c * 2 + h // 2) & (c == h % 2) & (zh == k)

    def fb_copy(h, d):
        xo, zo = (1 - xh if d // 4 else xh), zh_on[d % 4]
        q = xo * 4 + zo
        return rcopy(fb_send.at[h % 2, q], fb.at[xh * 4 + zh], fb_ss.at[h % 2, q],
                     fb_rs.at[xh * 4 + zh], dev(xl + 2 * xo, here, zl + 2 * zo, h % 2))

    def b_owner(h):
        return y == (1 - c) * 2 + h // 2

    def spread(h):
        a_copy(h).wait_recv()
        total = a_send[h, pl.ds(xh * 4, 4)].astype(F32) + a_recv[h].astype(F32)
        fa_send[h] = total.astype(BF16)
        for k in range(4):
            @pl.when(fa_self(h, k))
            def _(k=k):
                fa[y * 4 + zh] = fa_send[h, k]

            @pl.when(jnp.logical_not(fa_self(h, k)))
            def _(k=k):
                fa_copy(h, k).start()

        @pl.when(b_owner(h))
        def _():
            for slot in range(3):
                rcopy(b_send.at[h], b_recv.at[h % 2, slot], b_ss.at[h], b_rs.at[h % 2, slot],
                      dev(x, over, z, c)).wait_recv()
            t = b_send[h].astype(F32)
            for slot in range(3):
                t = t + b_recv[h % 2, slot].astype(F32)
            fb_send[h % 2] = t.astype(BF16)
            for d in (6, 5, 7, 4, 2, 1, 3):
                fb_copy(h, d).start()

            @pl.when(c != h % 2)
            def _():
                fb_copy(h, 0).start()

            @pl.when(c == h % 2)
            def _():
                fb[xh * 4 + zh] = fb_send[h % 2, xh * 4 + zh]

    def finish():
        own_a = yh == c
        for s in range(16):
            @pl.when(jnp.logical_not(own_a & (y * 4 + zh == s)))
            def _(s=s):
                rcopy(fb_send.at[0, 0], fa.at[s], fb_ss.at[0, 0], fa_rs.at[s], sibling).wait_recv()
        for s in range(8):
            @pl.when(own_a | (xh * 4 + zh != s))
            def _(s=s):
                rcopy(fb_send.at[0, 0], fb.at[s], fb_ss.at[0, 0], fb_rs.at[s], sibling).wait_recv()
        ta = fa[0].astype(F32)
        for s in range(1, 16):
            ta = ta + fa[s].astype(F32)
        tb = fb[0].astype(F32)
        for s in range(1, 8):
            tb = tb + fb[s].astype(F32)
        ta = ta * (1.0 / 64.0)
        tb = tb * (1.0 / 64.0)
        wk_ref[...] = jnp.where(yh == 0, ta, tb)
        wv_ref[...] = jnp.where(yh == 0, tb, ta)

    attention(0)
    for t in range(2):
        x_copy(t, 0).wait()
        start(x_forward(t, 0))
    attention(1)
    attention(2)
    finalize(0)
    attention(3)
    finalize(1)
    finalize(2)
    for m in (2, 1, 3):
        for t in range(2):
            x_copy(t, m).wait_recv()
            start(x_forward(t, m))
    finalize(3)
    for m in range(4):
        for t in range(2):
            x_forward(t, m).wait_recv()
    for h in range(KVH):
        gathered(h)
        product(h)
        if h > 1:
            spread(h - 2)
    spread(2)
    spread(3)
    finish()

    for cp in sends:
        cp.wait_send()
    for h in range(KVH):
        for delta in (1, 2):
            @pl.when(sq + delta < 4)
            def _(h=h, delta=delta):
                kv_copy(h, delta).wait_send()

            @pl.when(sq >= delta)
            def _(h=h, delta=delta):
                part_copy(h, delta).wait_send()

        @pl.when(jnp.logical_not(b_owner(h)))
        def _(h=h):
            b_copy(h).wait_send()

        for k in range(4):
            @pl.when(jnp.logical_not(fa_self(h, k)))
            def _(h=h, k=k):
                fa_copy(h, k).wait_send()

        @pl.when(b_owner(h))
        def _(h=h):
            for d in range(1, 8):
                fb_copy(h, d).wait_send()

            @pl.when(c != h % 2)
            def _():
                fb_copy(h, 0).wait_send()


def per_device(layer_input, query_states, key_states, value_states, output_grads, doc_lengths):
    hbm = pl.BlockSpec(memory_space=pltpu.HBM)
    vmem = pl.BlockSpec(memory_space=pltpu.VMEM)
    dma = pltpu.SemaphoreType.DMA
    dq, wk, wv = pl.pallas_call(
        kernel,
        out_shape=(
            jax.ShapeDtypeStruct((TOK, KVH * GROUP * HD), BF16),
            jax.ShapeDtypeStruct((ROWS, HD), F32),
            jax.ShapeDtypeStruct((ROWS, HD), F32),
        ),
        in_specs=[pl.BlockSpec(memory_space=pltpu.SMEM)] + [hbm] * 5,
        out_specs=(vmem, vmem, vmem),
        scratch_shapes=[
            pltpu.VMEM((TOK, D), BF16),
            pltpu.VMEM((TOK, KVH * GROUP * HD), BF16),
            pltpu.VMEM((TOK, KVH * GROUP * HD), BF16),
            pltpu.VMEM((KVH, 2, 3 * TOK, HD), BF16),
            pltpu.VMEM((TOK, 3 * TOK), F32),
            pltpu.VMEM((D, TOK), BF16),
            pltpu.VMEM((2, 8, 2, 4, ROWS, TOK), BF16),
            pltpu.VMEM((KVH, 2, HD, TOK), F32),
            pltpu.VMEM((KVH, 2, 2, HD, TOK), BF16),
            pltpu.VMEM((KVH, 2, 2, HD, TOK), BF16),
            pltpu.VMEM((KVH, 2, TOK, HD), BF16),
            pltpu.VMEM((2, KVH, 8 * TOK, HD), BF16),
            pltpu.VMEM((KVH, 8, ROWS, HD), BF16),
            pltpu.VMEM((KVH, 4, ROWS, HD), BF16),
            pltpu.VMEM((KVH, 8, ROWS, HD), BF16),
            pltpu.VMEM((2, 3, 8, ROWS, HD), BF16),
            pltpu.VMEM((KVH, 4, ROWS, HD), BF16),
            pltpu.VMEM((2, 8, ROWS, HD), BF16),
            pltpu.VMEM((16, ROWS, HD), BF16),
            pltpu.VMEM((8, ROWS, HD), BF16),
            dma((11,)),
            dma((KVH, 2)), dma((KVH, 2)),
            dma((2, 3)), dma((2, 3)), dma((2,)),
            dma((2, 4)), dma((2, 4)),
            dma((KVH, 2)), dma((KVH, 2)),
            dma((KVH, 2, 2, 4)), dma((KVH, 2, 4, 2)),
            dma((KVH,)), dma((KVH,)),
            dma((KVH,)), dma((2, 3)),
            dma((KVH, 4)), dma((16,)),
            dma((2, 8)), dma((8,)),
        ],
        compiler_params=pltpu.CompilerParams(
            collective_id=0, has_side_effects=True, vmem_limit_bytes=40 * 1024 * 1024,
        ),
        cost_estimate=pl.CostEstimate(
            flops=2_600_000_000, bytes_accessed=4_000_000, transcendentals=1_000_000),
    )(pltpu.with_memory_space_constraint(doc_lengths, pltpu.HBM), *[pltpu.with_memory_space_constraint(a[0], pltpu.HBM) for a in (
        layer_input, query_states, key_states, value_states, output_grads)])
    return dq[None], wk, wv


def solution(mesh):
    return jax.shard_map(
        per_device,
        mesh=mesh,
        in_specs=(
            P("dp", "seq", None),
            P("dp", "seq", None),
            P("dp", "seq", None),
            P("dp", "seq", None),
            P("dp", "seq", None),
            P("dp", None),
        ),
        out_specs=(P("dp", "seq", None), P("dp", "seq"), P("dp", "seq")),
        check_vma=False,
    )
```

time: 57.7 us -> 55.9 us (0.969)
  Pallas kernels: 54.9 us -> 53 us
    pallas_call x1, Pallas kernels: 54.9 us -> 53 us  [per_device(): pl.pallas_call(kernel, out_shape=(jax.ShapeDtypeStruct((TOK, KVH * GROUP...]
where the time goes in v3:
time: 55.9 us; the launch traced here: 55.8 us
  Pallas kernels  53 us (95%)
  local copies, waits for them, and re-layouts  2.07 us (4%)
  between operations  0.64 us (1%)
    pallas_call x1, Pallas kernels, per_device(): pl.pallas_call(kernel, out_shape=(jax.ShapeDtypeStruct((TOK, KVH * GROUP...  53 us
    unnamed x3, local copies, waits for them, and re-layouts  2.07 us

profile of v3, /device:TPU:9, one launch (start us, length us, event | category | flops | bytes accessed | tf_op | source)
XLA Modules:
  0.0 55.8 jit_solution(6027623289808578710)
XLA Ops:
  0.6 53.0 %shard_map.85 = (bf16[128,2560]{1,0:T(8,128)(2,1)S(1)}, f32[80,128]{1,0:T(8,128)S(1)}, f32[80,128]{1,0:T(8,128)S(1)}) custom-call(s32[1,6]{1,0:T(1,128)} %doc_ref.1, bf16[128,5120]{1,0:T(8,128)(2,1)} %bitcast.7, bf16[128,2560]{1,0:T(8,128)(2,1)} %bitcast.8, bf16[128,512]{1,0:T(8,128)(2,1)} %bitcast.10, bf16[128,512]{1,0:T(8,128)(2,1)} %bitcast.11, ...), custom_call_target="tpu_custom_call" | custom-call | flops 2600000000 | bytes 4000000 | tf_op jit(solution)/shard_map/pallas_call | solution.py:404
  53.7 0.8 %copy.12 = bf16[1,128,2560]{2,1,0:T(8,128)(2,1)} copy(bf16[1,128,2560]{2,1,0:T(8,128)(2,1)S(1)} %bitcast.6) | data formatting | bytes 1310720
  54.5 0.6 %copy.13 = f32[80,128]{1,0:T(8,128)} copy(f32[80,128]{1,0:T(8,128)S(1)} %get-tuple-element.13) | data formatting | bytes 81920
  55.1 0.6 %copy.14 = f32[80,128]{1,0:T(8,128)} copy(f32[80,128]{1,0:T(8,128)S(1)} %get-tuple-element.14) | data formatting | bytes 81920

commit v4 on v3

--- a/solution.py
+++ b/solution.py
@@ -22,12 +22,12 @@
 
 def kernel(
     doc_ref, x_hbm, q_hbm, k_hbm, v_hbm, do_hbm,
-    dq_ref, wk_ref, wv_ref,
+    dq_ref, w_ref,
     xin, qin, doin, kv, bias, xt_send, xt_all,
     part_own, part_send, part_recv, kvout, kv_all, a_send, a_recv, b_send, b_recv,
     fa_send, fb_send, fa, fb,
     ld_sem, kv_ss, kv_rs, x_ss, x_rs, xl_sem, xf_ss, xf_rs, p_ss, p_rs,
-    ag_ss, ag_rs, a_ss, a_rs, b_ss, b_rs, fa_ss, fa_rs, fb_ss, fb_rs,
+    ag_ss, ag_rs, a_ss, a_rs, b_ss, b_rs, fa_ss, fa_rs, fb_ss, fb_rs, met,
 ):
     dp = lax.axis_index("dp")
     sq = lax.axis_index("seq")
@@ -35,10 +35,14 @@
     x, z, yh = div(dp, 16), rem(div(dp, 2), 8), rem(dp, 2)
     yl, c = div(sq, 2), rem(sq, 2)
     y = yh * 2 + yl
-    xl, xh, zl, zh = rem(x, 2), div(x, 2), rem(z, 2), div(z, 2)
+    xl, v, zl, zh = rem(x, 2), div(x, 2), rem(z, 2), div(z, 2)
+    u = xl + v - 2 * xl * v
+    pair = (u, v)
+    rest_a, rest_b = v + (u - v) * c, u + (v - u) * c
     x_next = (x + 1 - 2 * xl, rem(x + 3 + 2 * xl, NX))
     z_next = (z + 1 - 2 * zl, rem(z + 7 + 2 * zl, NZ))
-    x_two = rem(x + 2, NX)
+    x_a = x_next[1] + (x_next[0] - x_next[1]) * c
+    x_b = x_next[0] + (x_next[1] - x_next[0]) * c
     zh_on = [zh] + [rem(zh + k, 4) for k in (1, 2, 3)]
     z_on = [zl + 2 * k for k in zh_on]
     ranks = [sq] + [rem(sq + k, 4) for k in (1, 2, 3)]
@@ -83,26 +87,28 @@
             peers += [dev(xx, here, zz, c), dev(xx, here, zz, 1 - c)]
     for k in (2, 1, 3, 0):
         zz = z_on[k]
-        places = [(x_two, here), (x, over), (x, beyond)]
+        places = [(x, over), (x, beyond)]
         if k > 0:
-            places += [(x, here), (x, across)]
+            places = [(x, here)]
         for xx, yy in places:
             peers += [dev(xx, yy, zz, c), dev(xx, yy, zz, 1 - c)]
     for peer in peers:
         pl.semaphore_signal(barrier, inc=1, device_id=peer, device_id_type=MESH)
 
-    def turn_block(xd):
+    def turn_block(ud, vd):
         def turn(i, _):
-            at = pl.multiple_of(xd * XW + i * 128, 128)
-            xt_send[pl.ds(at, 128), :] = xin[:, pl.ds(at, 128)].T
+            to = pl.multiple_of((2 * ud + vd) * XW + i * 128, 128)
+            at = pl.multiple_of((2 * vd + ud + vd - 2 * ud * vd) * XW + i * 128, 128)
+            xt_send[pl.ds(to, 128), :] = xin[:, pl.ds(at, 128)].T
             return 0
 
         lax.fori_loop(0, XW // 128, turn, 0)
 
     def x_copy(t, m):
         xx, zz = member(t, m)
-        xo, zo = (1 - xl if m // 2 else xl), (1 - zl if m % 2 else zl)
-        src = xt_send.reshape(2, 2, 4, 2, 2, ROWS, TOK).at[:, xo, :, zo, t]
+        xo, zo = (1 - pair[t] if m // 2 else pair[t]), (1 - zl if m % 2 else zl)
+        view = xt_send.reshape(2, 2, 4, 2, 2, ROWS, TOK)
+        src = view.at[:, xo, :, zo, t] if t else view.at[xo, :, :, zo, t]
         if m == 0:
             return pltpu.make_async_copy(src, xt_all.at[t, 0], xl_sem.at[t])
         return rcopy(src, xt_all.at[t, m * 2], x_ss.at[t, m - 1], x_rs.at[t, m - 1],
@@ -131,6 +137,8 @@
             @pl.when(sq + delta < 4)
             def _(h=h, delta=delta):
                 kv_copy(h, delta).start()
+    for xx, yy in ((x, over), (x, beyond), (x, across), (x_next[0], here), (x_next[1], here)):
+        pl.semaphore_signal(met, inc=1, device_id=dev(xx, yy, z, c), device_id_type=MESH)
     for delta in (1, 2):
         @pl.when(sq < delta)
         def _(delta=delta):
@@ -140,16 +148,17 @@
         def _(delta=delta):
             part_recv[:, delta - 1] = jnp.zeros((KVH, 2, HD, TOK), BF16)
     load_x.wait()
-    for part in (1, 0):
-        for half in range(2):
-            turn_block((1 - xl if part else xl) + 2 * half)
-        for t in range(2):
-            if part:
-                start(x_copy(t, 3))
-                start(x_copy(t, 2))
-            else:
-                start(x_copy(t, 1))
-                x_copy(t, 0).start()
+    turn_block(1 - u, v)
+    turn_block(1 - u, 1 - v)
+    start(x_copy(0, 3))
+    start(x_copy(0, 2))
+    turn_block(u, 1 - v)
+    start(x_copy(1, 3))
+    start(x_copy(1, 2))
+    turn_block(u, v)
+    for t in range(2):
+        start(x_copy(t, 1))
+        x_copy(t, 0).start()
 
     rows = lax.broadcasted_iota(jnp.int32, (TOK, 1), 0) + sq * TOK
     first = jnp.zeros((TOK, 1), jnp.int32)
@@ -260,8 +269,8 @@
                     b_copy(h).start()
 
     def a_copy(h):
-        src = a_send.reshape(KVH, 2, 4, ROWS, HD).at[h, 1 - xh]
-        return rcopy(src, a_recv.at[h], a_ss.at[h], a_rs.at[h], dev(x_two, here, z, c))
+        src = a_send.reshape(KVH, 2, 4, ROWS, HD).at[h, 1 - rest_a]
+        return rcopy(src, a_recv.at[h], a_ss.at[h], a_rs.at[h], dev(x_a, here, z, c))
 
     def b_copy(h):
         target = (1 - c) * 2 + h // 2
@@ -277,17 +286,18 @@
         return (y == c * 2 + h // 2) & (c == h % 2) & (zh == k)
 
     def fb_copy(h, d):
-        xo, zo = (1 - xh if d // 4 else xh), zh_on[d % 4]
+        xo, zo = (1 - rest_b if d // 4 else rest_b), zh_on[d % 4]
         q = xo * 4 + zo
-        return rcopy(fb_send.at[h % 2, q], fb.at[xh * 4 + zh], fb_ss.at[h % 2, q],
-                     fb_rs.at[xh * 4 + zh], dev(xl + 2 * xo, here, zl + 2 * zo, h % 2))
+        return rcopy(fb_send.at[h % 2, q], fb.at[rest_b * 4 + zh], fb_ss.at[h % 2, q],
+                     fb_rs.at[rest_b * 4 + zh],
+                     dev(x_b if d // 4 else x, here, zl + 2 * zo, h % 2))
 
     def b_owner(h):
         return y == (1 - c) * 2 + h // 2
 
     def spread(h):
         a_copy(h).wait_recv()
-        total = a_send[h, pl.ds(xh * 4, 4)].astype(F32) + a_recv[h].astype(F32)
+        total = a_send[h, pl.ds(rest_a * 4, 4)].astype(F32) + a_recv[h].astype(F32)
         fa_send[h] = total.astype(BF16)
         for k in range(4):
             @pl.when(fa_self(h, k))
@@ -316,7 +326,7 @@
 
             @pl.when(c == h % 2)
             def _():
-                fb[xh * 4 + zh] = fb_send[h % 2, xh * 4 + zh]
+                fb[rest_b * 4 + zh] = fb_send[h % 2, rest_b * 4 + zh]
 
     def finish():
         own_a = yh == c
@@ -325,7 +335,7 @@
             def _(s=s):
                 rcopy(fb_send.at[0, 0], fa.at[s], fb_ss.at[0, 0], fa_rs.at[s], sibling).wait_recv()
         for s in range(8):
-            @pl.when(own_a | (xh * 4 + zh != s))
+            @pl.when(own_a | (rest_b * 4 + zh != s))
             def _(s=s):
                 rcopy(fb_send.at[0, 0], fb.at[s], fb_ss.at[0, 0], fb_rs.at[s], sibling).wait_recv()
         ta = fa[0].astype(F32)
@@ -336,8 +346,8 @@
             tb = tb + fb[s].astype(F32)
         ta = ta * (1.0 / 64.0)
         tb = tb * (1.0 / 64.0)
-        wk_ref[...] = jnp.where(yh == 0, ta, tb)
-        wv_ref[...] = jnp.where(yh == 0, tb, ta)
+        w_ref[0] = jnp.where(yh == 0, ta, tb)
+        w_ref[1] = jnp.where(yh == 0, tb, ta)
 
     attention(0)
     for t in range(2):
@@ -357,6 +367,7 @@
     for m in range(4):
         for t in range(2):
             x_forward(t, m).wait_recv()
+    pl.semaphore_wait(met, 5)
     for h in range(KVH):
         gathered(h)
         product(h)
@@ -364,8 +375,6 @@
             spread(h - 2)
     spread(2)
     spread(3)
-    finish()
-
     for cp in sends:
         cp.wait_send()
     for h in range(KVH):
@@ -395,21 +404,21 @@
             @pl.when(c != h % 2)
             def _():
                 fb_copy(h, 0).wait_send()
+    finish()
 
 
 def per_device(layer_input, query_states, key_states, value_states, output_grads, doc_lengths):
     hbm = pl.BlockSpec(memory_space=pltpu.HBM)
     vmem = pl.BlockSpec(memory_space=pltpu.VMEM)
     dma = pltpu.SemaphoreType.DMA
-    dq, wk, wv = pl.pallas_call(
+    dq, w = pl.pallas_call(
         kernel,
         out_shape=(
             jax.ShapeDtypeStruct((TOK, KVH * GROUP * HD), BF16),
-            jax.ShapeDtypeStruct((ROWS, HD), F32),
-            jax.ShapeDtypeStruct((ROWS, HD), F32),
+            jax.ShapeDtypeStruct((2, ROWS, HD), F32),
         ),
         in_specs=[pl.BlockSpec(memory_space=pltpu.SMEM)] + [hbm] * 5,
-        out_specs=(vmem, vmem, vmem),
+        out_specs=(vmem, vmem),
         scratch_shapes=[
             pltpu.VMEM((TOK, D), BF16),
             pltpu.VMEM((TOK, KVH * GROUP * HD), BF16),
@@ -441,6 +450,7 @@
             dma((KVH,)), dma((2, 3)),
             dma((KVH, 4)), dma((16,)),
             dma((2, 8)), dma((8,)),
+            pltpu.SemaphoreType.REGULAR,
         ],
         compiler_params=pltpu.CompilerParams(
             collective_id=0, has_side_effects=True, vmem_limit_bytes=40 * 1024 * 1024,
@@ -449,7 +459,7 @@
             flops=2_600_000_000, bytes_accessed=4_000_000, transcendentals=1_000_000),
     )(pltpu.with_memory_space_constraint(doc_lengths, pltpu.HBM), *[pltpu.with_memory_space_constraint(a[0], pltpu.HBM) for a in (
         layer_input, query_states, key_states, value_states, output_grads)])
-    return dq[None], wk, wv
+    return dq[None], w[0], w[1]
 
 
 def solution(mesh):

time: 55.9 us -> 52.3 us (0.936)
  Pallas kernels: 53 us -> 49.6 us
  local copies, waits for them, and re-layouts: 2.07 us -> 1.47 us
    pallas_call x1, Pallas kernels: 53 us -> 49.6 us  [per_device(): pl.pallas_call(kernel, out_shape=(jax.ShapeDtypeStruct((TOK, KVH * GROUP...]
    unnamed x3 -> x1, local copies, waits for them, and re-layouts: 2.07 us -> 0.84 us
    squeeze x0 -> x1, local copies, waits for them, and re-layouts: none -> 0.64 us  [per_device(): return (dq[None], w[0], w[1])]
where the time goes in v4:
time: 52.3 us; the launch traced here: 51.7 us
  Pallas kernels  49.6 us (95%)
  local copies, waits for them, and re-layouts  1.47 us (3%)
  between operations  0.64 us (1%)
    pallas_call x1, Pallas kernels, per_device(): pl.pallas_call(kernel, out_shape=(jax.ShapeDtypeStruct((TOK, KVH * GROUP...  49.6 us

profile of v4, /device:TPU:9, one launch (start us, length us, event | category | flops | bytes accessed | tf_op | source)
XLA Modules:
  0.0 51.7 jit_solution(8473094010292112105)
XLA Ops:
  0.6 49.6 %shard_map.85 = (bf16[128,2560]{1,0:T(8,128)(2,1)S(1)}, f32[2,80,128]{2,1,0:T(8,128)S(1)}) custom-call(s32[1,6]{1,0:T(1,128)} %doc_ref.1, bf16[128,5120]{1,0:T(8,128)(2,1)} %bitcast.11, bf16[128,2560]{1,0:T(8,128)(2,1)} %bitcast.12, bf16[128,512]{1,0:T(8,128)(2,1)} %bitcast.14, bf16[128,512]{1,0:T(8,128)(2,1)} %bitcast.15, bf16[128,2560]{1,0:T(8,128)(2,1)} %bitcast.13), custom_call_target="tpu_custom_call" | custom-call | flops 2600000000 | bytes 4000000 | tf_op jit(solution)/shard_map/pallas_call | solution.py:414
  50.2 0.6 %slice_bitcast_fusion = (f32[80,128]{1,0:T(8,128)}, f32[80,128]{1,0:T(8,128)}) fusion(f32[2,80,128]{2,1,0:T(8,128)S(1)} %get-tuple-element.6), kind=kLoop, calls=%fused_computation | loop fusion | bytes 163840 | tf_op jit(solution)/shard_map/squeeze | solution.py:462
  50.9 0.8 %copy.10 = bf16[1,128,2560]{2,1,0:T(8,128)(2,1)} copy(bf16[1,128,2560]{2,1,0:T(8,128)(2,1)S(1)} %bitcast.10) | data formatting | bytes 1310720

commit v5 on v4

--- a/solution.py
+++ b/solution.py
@@ -12,6 +12,7 @@
 D = 5120
 XW = D // 4
 NX, NY, NZ = 4, 4, 8
+ORDER = (1, 2, 0, 3)
 ROWS = 80
 LOG2E = 1.4426950408889634
 SCALE = HD ** (-0.5)
@@ -132,7 +133,7 @@
         return rcopy(kv.at[h, :, 256:384], kv.at[h, :, (2 - delta) * TOK:(3 - delta) * TOK],
                      kv_ss.at[h, delta - 1], kv_rs.at[h, delta - 1], seq_dev(delta))
 
-    for h in range(KVH):
+    for h in ORDER:
         for delta in (2, 1):
             @pl.when(sq + delta < 4)
             def _(h=h, delta=delta):
@@ -349,16 +350,16 @@
         w_ref[0] = jnp.where(yh == 0, ta, tb)
         w_ref[1] = jnp.where(yh == 0, tb, ta)
 
-    attention(0)
+    attention(1)
     for t in range(2):
         x_copy(t, 0).wait()
         start(x_forward(t, 0))
-    attention(1)
     attention(2)
+    attention(0)
+    finalize(1)
+    attention(3)
+    finalize(2)
     finalize(0)
-    attention(3)
-    finalize(1)
-    finalize(2)
     for m in (2, 1, 3):
         for t in range(2):
             x_copy(t, m).wait_recv()
@@ -368,12 +369,12 @@
         for t in range(2):
             x_forward(t, m).wait_recv()
     pl.semaphore_wait(met, 5)
-    for h in range(KVH):
+    for n, h in enumerate(ORDER):
         gathered(h)
         product(h)
-        if h > 1:
-            spread(h - 2)
-    spread(2)
+        if n > 1:
+            spread(ORDER[n - 2])
+    spread(0)
     spread(3)
     for cp in sends:
         cp.wait_send()

time: 52.3 us -> 51.9 us (level)
  no operation moved by 1% of the time
where the time goes in v5:
time: 51.9 us; the launch traced here: 51.7 us
  Pallas kernels  49.6 us (96%)
  local copies, waits for them, and re-layouts  1.47 us (3%)
  between operations  0.64 us (1%)
    pallas_call x1, Pallas kernels, per_device(): pl.pallas_call(kernel, out_shape=(jax.ShapeDtypeStruct((TOK, KVH * GROUP...  49.6 us

profile of v5, /device:TPU:9, one launch (start us, length us, event | category | flops | bytes accessed | tf_op | source)
XLA Modules:
  0.0 51.7 jit_solution(12401368609474803867)
XLA Ops:
  0.6 49.6 %shard_map.85 = (bf16[128,2560]{1,0:T(8,128)(2,1)S(1)}, f32[2,80,128]{2,1,0:T(8,128)S(1)}) custom-call(s32[1,6]{1,0:T(1,128)} %doc_ref.1, bf16[128,5120]{1,0:T(8,128)(2,1)} %bitcast.11, bf16[128,2560]{1,0:T(8,128)(2,1)} %bitcast.12, bf16[128,512]{1,0:T(8,128)(2,1)} %bitcast.14, bf16[128,512]{1,0:T(8,128)(2,1)} %bitcast.15, bf16[128,2560]{1,0:T(8,128)(2,1)} %bitcast.13), custom_call_target="tpu_custom_call" | custom-call | flops 2600000000 | bytes 4000000 | tf_op jit(solution)/shard_map/pallas_call | solution.py:415
  50.2 0.6 %slice_bitcast_fusion = (f32[80,128]{1,0:T(8,128)}, f32[80,128]{1,0:T(8,128)}) fusion(f32[2,80,128]{2,1,0:T(8,128)S(1)} %get-tuple-element.6), kind=kLoop, calls=%fused_computation | loop fusion | bytes 163840 | tf_op jit(solution)/shard_map/squeeze | solution.py:463
  50.9 0.8 %copy.10 = bf16[1,128,2560]{2,1,0:T(8,128)(2,1)} copy(bf16[1,128,2560]{2,1,0:T(8,128)(2,1)S(1)} %bitcast.10) | data formatting | bytes 1310720

commit v6 on v5

--- a/solution.py
+++ b/solution.py
@@ -86,7 +86,7 @@
         for m in (3, 2, 1):
             xx, zz = member(t, m)
             peers += [dev(xx, here, zz, c), dev(xx, here, zz, 1 - c)]
-    for k in (2, 1, 3, 0):
+    for k in (1, 3, 0):
         zz = z_on[k]
         places = [(x, over), (x, beyond)]
         if k > 0:
@@ -138,8 +138,11 @@
             @pl.when(sq + delta < 4)
             def _(h=h, delta=delta):
                 kv_copy(h, delta).start()
-    for xx, yy in ((x, over), (x, beyond), (x, across), (x_next[0], here), (x_next[1], here)):
-        pl.semaphore_signal(met, inc=1, device_id=dev(xx, yy, z, c), device_id_type=MESH)
+    ahead, behind = dev(x, here, z_on[1], c), dev(x, here, z_on[3], c)
+    close = [dev(xx, yy, z, c) for xx, yy in
+             ((x, over), (x, beyond), (x, across), (x_next[0], here), (x_next[1], here))]
+    for device in close + [ahead, behind]:
+        pl.semaphore_signal(met.at[0], inc=1, device_id=device, device_id_type=MESH)
     for delta in (1, 2):
         @pl.when(sq < delta)
         def _(delta=delta):
@@ -356,19 +359,22 @@
         start(x_forward(t, 0))
     attention(2)
     attention(0)
+    pl.semaphore_wait(met.at[0], 7)
+    for device in (ahead, behind):
+        pl.semaphore_signal(met.at[1], inc=1, device_id=device, device_id_type=MESH)
     finalize(1)
     attention(3)
     finalize(2)
     finalize(0)
+    finalize(3)
     for m in (2, 1, 3):
         for t in range(2):
             x_copy(t, m).wait_recv()
             start(x_forward(t, m))
-    finalize(3)
     for m in range(4):
         for t in range(2):
             x_forward(t, m).wait_recv()
-    pl.semaphore_wait(met, 5)
+    pl.semaphore_wait(met.at[1], 2)
     for n, h in enumerate(ORDER):
         gathered(h)
         product(h)
@@ -451,7 +457,7 @@
             dma((KVH,)), dma((2, 3)),
             dma((KVH, 4)), dma((16,)),
             dma((2, 8)), dma((8,)),
-            pltpu.SemaphoreType.REGULAR,
+            pltpu.SemaphoreType.REGULAR((2,)),
         ],
         compiler_params=pltpu.CompilerParams(
             collective_id=0, has_side_effects=True, vmem_limit_bytes=40 * 1024 * 1024,

time: 51.9 us -> 52 us (level)
  no operation moved by 1% of the time
where the time goes in v6:
time: 52 us; the launch traced here: 51.9 us
  Pallas kernels  49.8 us (96%)
  local copies, waits for them, and re-layouts  1.47 us (3%)
  between operations  0.64 us (1%)
    pallas_call x1, Pallas kernels, per_device(): pl.pallas_call(kernel, out_shape=(jax.ShapeDtypeStruct((TOK, KVH * GROUP...  49.8 us

profile of v6, /device:TPU:9, one launch (start us, length us, event | category | flops | bytes accessed | tf_op | source)
XLA Modules:
  0.0 51.9 jit_solution(17334662298644373765)
XLA Ops:
  0.6 49.8 %shard_map.85 = (bf16[128,2560]{1,0:T(8,128)(2,1)S(1)}, f32[2,80,128]{2,1,0:T(8,128)S(1)}) custom-call(s32[1,6]{1,0:T(1,128)} %doc_ref.1, bf16[128,5120]{1,0:T(8,128)(2,1)} %bitcast.11, bf16[128,2560]{1,0:T(8,128)(2,1)} %bitcast.12, bf16[128,512]{1,0:T(8,128)(2,1)} %bitcast.14, bf16[128,512]{1,0:T(8,128)(2,1)} %bitcast.15, bf16[128,2560]{1,0:T(8,128)(2,1)} %bitcast.13), custom_call_target="tpu_custom_call" | custom-call | flops 2600000000 | bytes 4000000 | tf_op jit(solution)/shard_map/pallas_call | solution.py:421
  50.5 0.6 %slice_bitcast_fusion = (f32[80,128]{1,0:T(8,128)}, f32[80,128]{1,0:T(8,128)}) fusion(f32[2,80,128]{2,1,0:T(8,128)S(1)} %get-tuple-element.6), kind=kLoop, calls=%fused_computation | loop fusion | bytes 163840 | tf_op jit(solution)/shard_map/squeeze | solution.py:469
  51.1 0.8 %copy.10 = bf16[1,128,2560]{2,1,0:T(8,128)(2,1)} copy(bf16[1,128,2560]{2,1,0:T(8,128)(2,1)S(1)} %bitcast.10) | data formatting | bytes 1310720
